TPU v7x, 1024 devices: a whole 4x8x16 slice. The times are simulated.
1024 devices in a mesh: region: 16 (over z), tile: 64 (over x, y, core).
Axes of the slice: x: 4, y: 8, z: 16, core: 2. Of those that a mesh axis runs over, the one named last changes fastest.
Arguments:
- atm_state: bfloat16 [16384, 1280], P(('region', 'tile')), may hold values from -8 to 8
- ocean_state: float32 [65536, 512], P(('region', 'tile')), may hold values from -6 to 6
- cell_area: float32 [65536, 128], P(('region', 'tile')), may hold values from 1 to 10
- level_weights: float32 [4], replicated, may hold values from 0.1 to 1
- remap: bfloat16 [262144, 32, 128], P(('region', 'tile')), may hold values from 0.0019989014 to 0.059814453
- send_src: int32 [1024, 64, 4], P(('region', 'tile')), may hold values from -1 to 15, as said below
- recv_ocn: int32 [1024, 64, 4], P(('region', 'tile')), may hold values from -1 to 63, as said below
Outputs:
- ocean_flux: float32 [65536, 1024], P(('region', 'tile'))
- atm_flux: float32 [16384, 256], P(('region', 'tile'))
Inputs may be any that keep to these rules, and one draw needn't show every extreme that they name: `send_src`: each device fills exactly 128 of its slots; in every region 8 ocean partitions, drawn from the seed, receive all 4 slots from every sender; other entries are -1. `recv_ocn`: an entry is -1 exactly where the matching entry of send_src (sender and receiver exchanged) is -1.
All inputs are finite; a program needn't handle non-finite values.
Results may differ from a plain program's by a relative error of at most 0.0019.
Values may be sent and summed in bfloat16 or wider, within the bound.
A program may use at most 32 MiB of HBM per device.

v0:
```python
import jax
import jax.numpy as jnp
from jax import lax
from jax.sharding import PartitionSpec as P


def bulk_fluxes(remapped, ocean, level_weights):
    block_count = remapped.shape[0]
    cells = remapped.shape[2]
    depth = level_weights.shape[0]
    fields = remapped.reshape(block_count, remapped.shape[1] // depth, depth, cells)
    bottom = jnp.einsum("kflo,l->kfo", fields, level_weights, precision=lax.Precision.HIGHEST)
    surface = ocean.reshape(block_count, 4, cells)
    wind_x = bottom[:, 0] - surface[:, 1]
    wind_y = bottom[:, 1] - surface[:, 2]
    speed = jnp.sqrt(wind_x * wind_x + wind_y * wind_y + bottom[:, 9] * bottom[:, 9] + 1.0)
    transfer = 0.1 * jnp.exp(0.2 * jnp.tanh(bottom[:, 8])) * speed
    stress_x = transfer * wind_x
    stress_y = transfer * wind_y
    sensible = transfer * (bottom[:, 2] - surface[:, 0])
    saturated = jnp.exp(0.1 * surface[:, 0] - 0.1 * jnp.tanh(bottom[:, 7]))
    latent = transfer * (bottom[:, 3] - saturated)
    albedo = 0.05 + 0.3 * jax.nn.sigmoid(surface[:, 3])
    shortwave = (1.0 - albedo) * jax.nn.softplus(bottom[:, 4])
    longwave = jax.nn.softplus(bottom[:, 5]) - 1.0 - 0.2 * surface[:, 0]
    freshwater = jax.nn.softplus(bottom[:, 6]) + latent
    heating = sensible + latent + shortwave + longwave
    return jnp.stack(
        [stress_x, stress_y, sensible, latent, shortwave, longwave, freshwater, heating], axis=1
    )


def per_device(atm_state, ocean_state, cell_area, level_weights, remap, send_src, recv_ocn):
    tile_count = lax.axis_size("tile")
    slot_depth = send_src.shape[2]
    slot_count = tile_count * slot_depth
    atm_blocks = atm_state.shape[0]
    row_width = atm_state.shape[1]
    columns = remap.shape[1]
    channels = row_width // columns
    ocean_blocks = ocean_state.shape[0]
    owner_ocean = recv_ocn.reshape(slot_count)
    sources = lax.all_gather(send_src, "tile", axis=0, tiled=True)
    own_index = lax.axis_index("tile")
    incoming = lax.dynamic_index_in_dim(sources, own_index, 1, keepdims=False).reshape(slot_count)
    piece = lax.all_gather(atm_state, "tile", axis=0, tiled=True)
    senders_here = piece.shape[0] // atm_blocks
    width = senders_here * slot_depth
    local_rows = jnp.arange(width, dtype=jnp.int32) // slot_depth * atm_blocks + jnp.maximum(
        incoming, 0
    )
    fetched = jnp.take(piece, local_rows, axis=0)
    fetched = jnp.where((incoming >= 0)[:, None], fetched, jnp.zeros_like(fetched))
    contrib = jnp.einsum(
        "scb,sbo->sco",
        fetched.reshape(slot_count, channels, columns),
        remap,
        preferred_element_type=jnp.float32,
    )
    selector = (owner_ocean[:, None] == jnp.arange(ocean_blocks, dtype=jnp.int32)[None, :]).astype(
        jnp.float32
    )
    remapped = jnp.einsum("sk,sco->kco", selector, contrib, precision=lax.Precision.HIGHEST)
    raw_flux = bulk_fluxes(remapped, ocean_state, level_weights)
    weighted = jnp.sum(cell_area * raw_flux[:, 6, :])
    area_total = jnp.sum(cell_area)
    totals = lax.psum((weighted, area_total), ("region", "tile"))
    shift = totals[0] / totals[1]
    corrected = raw_flux.at[:, 6, :].add(-shift)
    flux_fields = corrected.shape[1]
    ocean_flux = corrected.reshape(ocean_blocks, flux_fields * corrected.shape[2])
    rounded = corrected.astype(jnp.bfloat16)
    rows_back = jnp.take(rounded, jnp.maximum(owner_ocean, 0), axis=0)
    rows_back = jnp.where((owner_ocean >= 0)[:, None, None], rows_back, jnp.zeros_like(rows_back))
    back = jnp.einsum("sfo,sbo->sfb", rows_back, remap, preferred_element_type=jnp.float32).astype(
        jnp.bfloat16
    )
    returned = lax.all_to_all(
        back.reshape(tile_count, slot_depth, flux_fields * columns),
        "tile",
        split_axis=0,
        concat_axis=0,
        tiled=True,
    )
    returned = returned.reshape(slot_count, flux_fields * columns)
    owner_atm = send_src[0].reshape(slot_count)
    gather_atm = (owner_atm[:, None] == jnp.arange(atm_blocks, dtype=jnp.int32)[None, :]).astype(
        jnp.bfloat16
    )
    atm_flux = jnp.dot(gather_atm.T, returned, preferred_element_type=jnp.float32)
    return (ocean_flux, atm_flux)


def solution(mesh):
    in_specs = (
        P(("region", "tile"), None),
        P(("region", "tile"), None),
        P(("region", "tile"), None),
        P(),
        P(("region", "tile"), None, None),
        P(("region", "tile"), None, None),
        P(("region", "tile"), None, None),
    )
    out_specs = (P(("region", "tile"), None), P(("region", "tile"), None))
    return jax.shard_map(
        per_device, mesh=mesh, in_specs=in_specs, out_specs=out_specs, check_vma=False
    )
```

profile of v0, /device:TPU:1, one launch (start us, length us, event | category | flops | bytes accessed | tf_op | source)
XLA Modules:
  0.0 290.1 jit_solution(1388685549175537191)
XLA Ops:
  7.2 0.0 copy-start
  7.2 0.0 all-gather.2.cloned.1.call-start
  7.2 0.7 all-gather.2.cloned.1.call-update
  7.9 61.0 %all_gather.6 = s32[64,64,4]{1,2,0:T(4,128)S(1)} all-gather(s32[1,64,4]{1,2,0:T(4,128)} %param.14), channel_id=1, replica_groups=mesh['region'=16,'tile'=64] {'tile'}, dimensions={0}, use_global_device_ids=true | all-gather | bytes 66560 | tf_op jit(solution)/shard_map/all_gather | solution.py:43
  69.0 1.2 maximum_reduce_fusion
  70.2 0.1 max.62
  70.3 0.1 max.61
  70.4 1.3 compare_reduce_fusion
  71.7 0.1 ge.34
  71.8 0.8 copy.74
  72.6 0.1 eq.30
  72.7 1.0 reshape.183
  73.7 0.7 broadcast_maximum_fusion
  74.3 0.1 copy.84
  74.4 0.1 reshape.203
  74.6 0.6 broadcast_compare_fusion
  75.2 0.1 fusion.49
  75.3 40.2 %all-gather.2.cloned.1.call-done = bf16[1024,1280]{1,0:T(8,128)(2,1)} async-done(((bf16[16,1280]{1,0:T(8,128)(2,1)}), bf16[1024,1280]{1,0:T(8,128)(2,1)}) %all-gather.2.cloned.1.call-update) | async-done | bytes 2621456 | tf_op jit(solution)/shard_map/all_gather | solution.py:46
  115.5 3.9 %gather_fusion = bf16[256,1280]{1,0:T(8,128)(2,1)S(1)} fusion(bf16[1024,1280]{1,0:T(8,128)(2,1)} %all-gather.2.cloned.1.call-done, s32[1024]{0:T(1024)S(1)} %pad_clamp_fusion.1), kind=kCustom, calls=%fused_computation | custom fusion | bytes 1311744 | tf_op jit(solution)/shard_map/jit(_take)/gather | solution.py:52
  119.3 0.2 copy.75
  119.6 0.1 select_select_fusion
  119.7 4.5 %copy.76 = bf16[256,40,32]{1,2,0:T(8,128)(2,1)} copy(bf16[256,40,32]{0,2,1:T(8,128)(2,1)S(1)} %select_select_fusion) | data formatting | bytes 1310720 | tf_op jit(solution)/shard_map/jit(_where)/select_n | solution.py:53
  124.2 0.0 copy-done
  124.2 3.1 %fusion.50 = f32[256,40,128]{2,1,0:T(8,128)S(1)} fusion(bf16[256,40,32]{1,2,0:T(8,128)(2,1)} %copy.76, bf16[256,32,128]{2,1,0:T(8,128)(2,1)S(1)} %copy-done), kind=kOutput, calls=%fused_computation.94 | convolution fusion | flops 83886080 | bytes 7995392 | tf_op jit(solution)/shard_map/scb,sbo->sco/dot_general | solution.py:54
  127.3 0.0 copy-start.3
  127.3 2.5 fusion
  129.9 0.0 copy-done.3
  129.9 3.1 %fusion.2 = f32[1,64,10,128]{3,0,2,1:T(1,128)S(1)} fusion(f32[64,10,4,128]{3,0,2,1:T(8,128)S(1)} %bitcast.45, f32[4]{0:T(128)S(1)} %copy-done.3), kind=kOutput, calls=%fused_computation.4 | convolution fusion | flops 3932160 | bytes 1638416 | tf_op jit(solution)/shard_map/kflo,l->kfo/dot_general | solution.py:12
  133.1 0.0 copy-start.4
  133.1 0.0 copy-start.5
  133.1 0.0 copy-done.1
  133.1 0.7 fusion.46
  133.8 123.1 %all-reduce = (f32[]{:T(128)}, f32[]{:T(128)}) all-reduce(f32[]{:T(128)} %get-tuple-element.15, f32[]{:T(128)} %get-tuple-element.14), channel_id=1, replica_groups=mesh['region'=16,'tile'=64] {'region','tile'}, use_global_device_ids=true, to_apply=%region_1.2 | all-reduce | flops 2 | bytes 16 | tf_op jit(solution)/shard_map/psum | solution.py:67
  258.4 0.1 add_dynamic-update-slice_fusion.1
  258.5 0.1 copy.85
  258.6 0.8 gather_fusion.1
  259.5 0.0 copy-done.4
  259.5 0.0 copy-done.5
  259.5 0.0 copy-start.2
  259.5 2.5 convolution_convert_fusion
  261.9 2.1 reshape.185
  264.0 8.0 %all-to-all-start = ((bf16[64,4,256]{2,1,0:T(4,128)(2,1)}), bf16[64,4,256]{2,1,0:T(4,128)(2,1)S(1)}, u32[]{:S(2)}, u32[]{:S(2)}) async-start(bf16[64,4,256]{2,1,0:T(4,128)(2,1)} %reshape.185), calls=%async_computation | async-start | bytes 262144 | tf_op jit(solution)/shard_map/all_to_all | solution.py:78
  272.0 0.0 copy-done.2
  272.0 0.1 copy.83
  272.1 0.1 eq.34
  272.2 0.7 copy_bitcast_fusion.1
  273.0 9.4 %all-to-all-done = bf16[64,4,256]{2,1,0:T(4,128)(2,1)S(1)} async-done(((bf16[64,4,256]{2,1,0:T(4,128)(2,1)}), bf16[64,4,256]{2,1,0:T(4,128)(2,1)S(1)}, u32[]{:S(2)}, u32[]{:S(2)}) %all-to-all-start) | async-done | bytes 131104 | tf_op jit(solution)/shard_map/all_to_all | solution.py:78
  282.4 0.9 fusion.10
  (16 shorter events, 0.3 us)
Async XLA Ops:
  7.2 117.0 %copy-start = (bf16[256,32,128]{2,1,0:T(8,128)(2,1)S(1)}, bf16[256,32,128]{2,1,0:T(8,128)(2,1)}, u32[]{:S(2)}) copy-start(bf16[256,32,128]{2,1,0:T(8,128)(2,1)} %param.13) | copy-start | bytes 6291460
  7.2 108.3 %all-gather.2.cloned.1.call-start = ((), (), s32[]{:S(2)}) async-start(), calls=%async_computation.1 | async-start | bytes 2662400 | tf_op jit(solution)/shard_map/all_gather | solution.py:46
  127.3 2.6 copy-start.3
  129.9 3.2 %copy-start.1 = (f32[64,128]{1,0:T(8,128)S(1)}, f32[64,128]{1,0:T(8,128)}, u32[]{:S(2)}) copy-start(f32[64,128]{1,0:T(8,128)} %param.11) | copy-start | bytes 98308
  133.1 126.4 %copy-start.4 = (pred[256]{0:T(512)(128)(4,1)S(1)}, pred[256]{0:T(512)(128)(4,1)}, u32[]{:S(2)}) copy-start(pred[256]{0:T(512)(128)(4,1)} %get-tuple-element.24) | copy-start | bytes 772
  133.1 126.4 %copy-start.5 = (pred[256]{0:T(512)(128)(4,1)S(1)}, pred[256]{0:T(512)(128)(4,1)}, u32[]{:S(2)}) copy-start(pred[256]{0:T(512)(128)(4,1)} %get-tuple-element.25) | copy-start | bytes 772
  259.5 12.6 %copy-start.2 = (s32[1,64,4]{1,2,0:T(4,128)S(1)}, s32[1,64,4]{1,2,0:T(4,128)}, u32[]{:S(2)}) copy-start(s32[1,64,4]{1,2,0:T(4,128)} %param.14) | copy-start | bytes 3076
  264.0 18.4 %all-to-all-start = ((bf16[64,4,256]{2,1,0:T(4,128)(2,1)}), bf16[64,4,256]{2,1,0:T(4,128)(2,1)S(1)}, u32[]{:S(2)}, u32[]{:S(2)}) async-start(bf16[64,4,256]{2,1,0:T(4,128)(2,1)} %reshape.185), calls=%async_computation | async-start | bytes 262144 | tf_op jit(solution)/shard_map/all_to_all | solution.py:78
Sparse Core Ops, SparseCore 0:
  12.5 102.9 all-gather.1
where the time goes:
time: 291 us; the launch traced here: 290 us
  blocking collectives  184 us (63%)
  waiting for transfers between devices  50.3 us (17%)
  between operations  15.7 us (5%)
  local copies, waits for them, and re-layouts  15 us (5%)
  matrix products  12.1 us (4%)
  starting transfers between devices  8.05 us (3%)
  other arithmetic  4.79 us (2%)
    psum x1, blocking collectives, per_device(): totals = lax.psum((weighted, area_total), ('region', 'tile'))  123 us
    all_gather x1, blocking collectives, per_device(): sources = lax.all_gather(send_src, 'tile', axis=0, tiled=True)  61 us
    all_gather x1, waiting for transfers between devices, per_device(): piece = lax.all_gather(atm_state, 'tile', axis=0, tiled=True)  40.2 us
    all_to_all x1, waiting for transfers between devices, per_device(): lax.all_to_all(back.reshape(tile_count, slot_depth, flux_fields * columns...  9.42 us
    all_to_all x1, starting transfers between devices, per_device(): lax.all_to_all(back.reshape(tile_count, slot_depth, flux_fields * columns...  8.01 us
  transfers between devices with their start and end apart: 2, of which 2 were waited for; matrix products, arithmetic and copies ran while one was open for 2% of the time, Pallas kernels for 0%

commit v1 on v0

v1 whole, which is shorter than its diff:
```python
import functools

import jax
import jax.numpy as jnp
from jax import lax
from jax.experimental import pallas as pl
from jax.experimental.pallas import tpu as pltpu
from jax.sharding import PartitionSpec as P

F32 = jnp.float32
BF16 = jnp.bfloat16
MESH = pl.DeviceIdType.MESH


def iota(shape, axis):
    return lax.broadcasted_iota(jnp.int32, shape, axis)


def two_parts(x):
    high = x.astype(BF16)
    return high, (x - high.astype(F32)).astype(BF16)


def dot(a, b, contract=((1,), (0,))):
    return lax.dot_general(a, b, (contract, ((), ())), preferred_element_type=F32)


def softplus(x):
    return jnp.maximum(x, 0.0) + jnp.log1p(jnp.exp(-jnp.abs(x)))


def fluxes(bottom, surface):
    sst, ocean_u, ocean_v, albedo_in = surface
    wind_x = bottom[0] - ocean_u
    wind_y = bottom[1] - ocean_v
    speed = jnp.sqrt(wind_x * wind_x + wind_y * wind_y + bottom[9] * bottom[9] + 1.0)
    transfer = 0.1 * jnp.exp(0.2 * jnp.tanh(bottom[8])) * speed
    stress_x = transfer * wind_x
    stress_y = transfer * wind_y
    sensible = transfer * (bottom[2] - sst)
    saturated = jnp.exp(0.1 * sst - 0.1 * jnp.tanh(bottom[7]))
    latent = transfer * (bottom[3] - saturated)
    albedo = 0.05 + 0.3 * (1.0 / (1.0 + jnp.exp(-albedo_in)))
    shortwave = (1.0 - albedo) * softplus(bottom[4])
    longwave = softplus(bottom[5]) - 1.0 - 0.2 * sst
    freshwater = softplus(bottom[6]) + latent
    heating = sensible + latent + shortwave + longwave
    return [stress_x, stress_y, sensible, latent, shortwave, longwave, freshwater, heating]


def kernel(
    regions, tiles, atm_ref, ocean_ref, area_ref, weights_ref, remap_ref, src_ref, owner_ref,
    ocean_out, atm_out,
    remap, send1, recv1, contrib, rows_back, send2, recv2, zrows,
    remap_sem, send1_sem, recv1_sem, send2_sem, recv2_sem, zsend_sem, zrecv_sem,
):
    region = lax.axis_index("region")
    tile = lax.axis_index("tile")
    cap = src_ref.shape[1]
    atm_blocks = atm_ref.shape[0]
    ocean_blocks, cells = area_ref.shape
    nf = atm_ref.shape[1] // cells
    columns = cells // cap
    slots = tiles * cap
    nflx = 8
    parts = slots // 8

    load_remap = pltpu.make_async_copy(remap_ref, remap, remap_sem)
    load_remap.start()

    barrier = pltpu.get_barrier_semaphore()

    @pl.loop(1, tiles)
    def _(i):
        peer = lax.rem(tile + i, tiles)
        pl.semaphore_signal(barrier, inc=1, device_id=(region, peer), device_id_type=MESH)

    @pl.loop(1, regions)
    def _(i):
        peer = lax.rem(region + i, regions)
        pl.semaphore_signal(barrier, inc=1, device_id=(peer, tile), device_id_type=MESH)

    lane = iota((atm_blocks, cells), 1)
    level = lane // columns
    level_weight = jnp.zeros((atm_blocks, cells), F32)
    for l in range(cap):
        level_weight = jnp.where(level == l, weights_ref[l], level_weight)
    pieces = []
    for f in range(nf):
        x = atm_ref[:, f * cells : (f + 1) * cells].astype(F32) * level_weight
        x = x + pltpu.roll(x, 2 * columns, 1)
        pieces.append(x + pltpu.roll(x, columns, 1))
    combined = jnp.concatenate(pieces, axis=1)
    block = iota((atm_blocks, nf * cells), 1) % cells // columns
    stacked = jnp.concatenate([jnp.where(block == c, combined, 0.0) for c in range(cap)], axis=0)
    first, rest = two_parts(stacked)
    second = rest
    remainder = stacked - first.astype(F32) - second.astype(F32)
    third = remainder.astype(BF16)
    table = jnp.concatenate([first, second, third], axis=0)
    width = 3 * cap * atm_blocks
    at = iota((width, tiles), 0)
    wanted = jnp.full((width, tiles), -1, jnp.int32)
    for c in range(cap):
        wanted = jnp.where(at // atm_blocks % cap == c, src_ref[0, c : c + 1, :], wanted)
    pick = jnp.where(wanted == at % atm_blocks, 1.0, 0.0).astype(BF16)
    packed = dot(pick, table, ((0,), (0,)))
    for f in range(nf):
        send1[:, f, :] = packed[:, f * cells : (f + 1) * cells]

    repeat = jnp.where(iota((tiles, slots), 1) // cap == iota((tiles, slots), 0), 1.0, 0.0)
    by_slot = dot(owner_ref[0].astype(F32).astype(BF16), repeat.astype(BF16))
    own_row = iota((cap, slots), 0) == iota((cap, slots), 1) % cap
    owner_of = jnp.sum(jnp.where(own_row, by_slot, 0.0), axis=0, keepdims=True)
    feeds = jnp.where(
        owner_of.astype(jnp.int32) == iota((ocean_blocks, slots), 0), 1.0, 0.0
    ).astype(BF16)

    pl.semaphore_wait(barrier, tiles - 1 + regions - 1)

    def exchange(source, target, send_sem, recv_sem):
        @pl.loop(1, tiles)
        def _(i):
            peer = lax.rem(tile + i, tiles)
            pltpu.make_async_remote_copy(
                src_ref=source.at[peer, pl.ds(0, nf)],
                dst_ref=target.at[tile, pl.ds(0, nf)],
                send_sem=send_sem,
                recv_sem=recv_sem,
                device_id=(region, peer),
                device_id_type=MESH,
            ).start()

        target[pl.ds(tile, 1), pl.ds(0, nf), :] = source[pl.ds(tile, 1), pl.ds(0, nf), :]

    def drain(buffer, sem):
        whole = buffer.at[pl.ds(0, tiles - 1), pl.ds(0, nf)]
        pltpu.make_async_copy(whole, whole, sem).wait()

    exchange(send1, recv1, send1_sem, recv1_sem)
    load_remap.wait()
    drain(recv1, recv1_sem)

    row8 = iota((8, cells), 0)
    lane8 = iota((8, cells), 1)
    diagonal = [
        (row8 // cap == h) & (row8 % cap == lane8 // columns) for h in range(8 // cap)
    ]

    @pl.loop(0, parts)
    def _(g):
        halves = []
        for h in range(8 // cap):
            j = g * (8 // cap) + h
            rows = [
                jnp.where(diagonal[h], jnp.broadcast_to(recv1[j, pl.ds(f, 1), :], (8, cells)), 0.0)
                for f in range(nf)
            ]
            halves.append(jnp.concatenate(rows, axis=0))
        high, low = two_parts(jnp.concatenate(halves, axis=1))
        w = remap[pl.ds(pl.multiple_of(g * 8 * columns, 8 * columns), 8 * columns), :]
        out = dot(high, w) + dot(low, w)
        for f in range(nf):
            contrib[pl.ds(pl.multiple_of(g * 8, 8), 8), f * cells : (f + 1) * cells] = out[
                f * 8 : (f + 1) * 8
            ]

    high, low = two_parts(contrib[...])
    bottom = dot(feeds, high) + dot(feeds, low)
    raw = fluxes(
        [bottom[:, f * cells : (f + 1) * cells] for f in range(nf)],
        [ocean_ref[:, f * cells : (f + 1) * cells] for f in range(4)],
    )
    fresh = raw[6]
    for f in range(nflx):
        if f != 6:
            ocean_out[:, f * cells : (f + 1) * cells] = raw[f]

    weighted = jnp.sum(area_ref[...] * fresh, axis=0, keepdims=True)
    total = jnp.sum(area_ref[...], axis=0, keepdims=True)
    half = cells // 2
    low_lanes = iota((1, cells), 1) < half
    sums = jnp.where(
        low_lanes, weighted + pltpu.roll(weighted, half, 1), total + pltpu.roll(total, half, 1)
    )
    zrows[pl.ds(region, 1), pl.ds(0, 1), :] = sums.reshape(1, 1, cells)

    @pl.loop(1, regions)
    def _(i):
        peer = lax.rem(region + i, regions)
        pltpu.make_async_remote_copy(
            src_ref=zrows.at[region, pl.ds(0, 1)],
            dst_ref=zrows.at[region, pl.ds(0, 1)],
            send_sem=zsend_sem,
            recv_sem=zrecv_sem,
            device_id=(peer, tile),
            device_id_type=MESH,
        ).start()

    fresh_high, fresh_low = two_parts(fresh)
    fields = [r.astype(BF16) for r in raw]
    fields[6] = fresh_high
    taken = dot(feeds, jnp.concatenate(fields + [fresh_low], axis=1), ((0,), (0,)))
    rows_back[...] = taken
    ones = jnp.ones((8, cells), F32)

    @pl.loop(0, parts)
    def _(g):
        at_rows = pl.ds(pl.multiple_of(g * 8, 8), 8)
        rows = [rows_back[at_rows, f * cells : (f + 1) * cells] for f in range(nflx + 1)]
        left = jnp.concatenate(rows + [ones], axis=0).astype(BF16)
        w = remap[pl.ds(pl.multiple_of(g * 8 * columns, 8 * columns), 8 * columns), :]
        out = dot(left, w, ((1,), (1,)))
        for h in range(8 // cap):
            j = g * (8 // cap) + h
            piece = out[:, h * cells : (h + 1) * cells]
            for f in range(nflx):
                x = piece[f * 8 : (f + 1) * 8]
                if f == 6:
                    x = x + piece[nflx * 8 : nflx * 8 + 8]
                send2[j, pl.ds(f, 1), :] = jnp.sum(
                    jnp.where(diagonal[h], x, 0.0), axis=0, keepdims=True
                )
            send2[j, pl.ds(nflx, 1), :] = piece[(nflx + 1) * 8 : (nflx + 1) * 8 + 1]

    if regions > 1:
        zs = zrows.at[pl.ds(0, regions - 1), pl.ds(0, 1)]
        pltpu.make_async_copy(zs, zs, zrecv_sem).wait()
    zsum = jnp.sum(zrows[:, 0, :], axis=0, keepdims=True)
    send2[:, nflx + 1, :] = jnp.broadcast_to(zsum, (tiles, cells))

    exchange(send2, recv2, send2_sem, recv2_sem)
    drain(recv2, recv2_sem)

    sums_all = jnp.sum(recv2[:, nflx + 1, :], axis=0, keepdims=True)
    weighted_all = jnp.sum(jnp.where(low_lanes, sums_all, 0.0), axis=1, keepdims=True)
    area_all = jnp.sum(jnp.where(low_lanes, 0.0, sums_all), axis=1, keepdims=True)
    shift = weighted_all / area_all
    ocean_out[:, 6 * cells : 7 * cells] = fresh - shift

    back = []
    for f in range(nflx):
        x = recv2[:, f, :]
        if f == 6:
            x = x - shift * recv2[:, nflx, :]
        back.append(x.astype(BF16))
    gathered = dot(pick[: cap * atm_blocks], jnp.concatenate(back, axis=1))
    group = iota((atm_blocks, cells), 1) // columns
    outs = []
    for f in range(nflx):
        x = jnp.zeros((atm_blocks, cells), F32)
        for c in range(cap):
            x = jnp.where(
                group == c,
                gathered[c * atm_blocks : (c + 1) * atm_blocks, f * cells : (f + 1) * cells],
                x,
            )
        x = x + pltpu.roll(x, 2 * columns, 1)
        outs.append(x + pltpu.roll(x, columns, 1))
    for t in range(nflx // cap):
        x = outs[t * cap]
        for c in range(1, cap):
            x = jnp.where(group == c, outs[t * cap + c], x)
        atm_out[:, t * cells : (t + 1) * cells] = x

    drain(send1, send1_sem)
    drain(send2, send2_sem)
    if regions > 1:
        zs = zrows.at[pl.ds(0, regions - 1), pl.ds(0, 1)]
        pltpu.make_async_copy(zs, zs, zsend_sem).wait()


def per_device(
    regions, tiles, atm_state, ocean_state, cell_area, level_weights, remap, send_src, recv_ocn
):
    cap = send_src.shape[2]
    slots = tiles * cap
    atm_blocks = atm_state.shape[0]
    ocean_blocks, cells = cell_area.shape
    columns = remap.shape[1]
    nf = atm_state.shape[1] // cells
    nflx = 8
    vmem = pl.BlockSpec(memory_space=pltpu.VMEM)
    box = pltpu.VMEM((tiles, 16, cells), F32)
    dma = pltpu.SemaphoreType.DMA
    return pl.pallas_call(
        functools.partial(kernel, regions, tiles),
        out_shape=(
            jax.ShapeDtypeStruct((ocean_blocks, nflx * cells), F32),
            jax.ShapeDtypeStruct((atm_blocks, nflx * columns), F32),
        ),
        in_specs=[
            vmem,
            vmem,
            vmem,
            pl.BlockSpec(memory_space=pltpu.SMEM),
            pl.BlockSpec(memory_space=pl.ANY),
            vmem,
            vmem,
        ],
        out_specs=(vmem, vmem),
        scratch_shapes=[
            pltpu.VMEM((slots * columns, cells), BF16),
            box,
            box,
            pltpu.VMEM((slots, nf * cells), F32),
            pltpu.VMEM((slots, (nflx + 1) * cells), F32),
            box,
            box,
            pltpu.VMEM((regions, 8, cells), F32),
            dma, dma, dma, dma, dma, dma, dma,
        ],
        compiler_params=pltpu.CompilerParams(
            collective_id=0, has_side_effects=True, vmem_limit_bytes=40 * 1024 * 1024
        ),
        cost_estimate=pl.CostEstimate(
            flops=400_000_000, bytes_accessed=4_000_000, transcendentals=100_000
        ),
        name="couple",
    )(
        atm_state, ocean_state, cell_area, level_weights,
        remap.reshape(slots * columns, cells),
        jnp.swapaxes(send_src, 1, 2), jnp.swapaxes(recv_ocn, 1, 2),
    )


def solution(mesh):
    in_specs = (
        P(("region", "tile"), None),
        P(("region", "tile"), None),
        P(("region", "tile"), None),
        P(),
        P(("region", "tile"), None, None),
        P(("region", "tile"), None, None),
        P(("region", "tile"), None, None),
    )
    out_specs = (P(("region", "tile"), None), P(("region", "tile"), None))
    return jax.shard_map(
        functools.partial(per_device, mesh.shape["region"], mesh.shape["tile"]),
        mesh=mesh,
        in_specs=in_specs,
        out_specs=out_specs,
        check_vma=False,
    )
```

time: 291 us -> 66.4 us (0.23)
  blocking collectives: 184 us -> 0 us
  Pallas kernels: 0 us -> 58 us
  waiting for transfers between devices: 50.3 us -> 0 us
  between operations: 15.7 us -> 0.66 us
  matrix products: 12.1 us -> 0 us
  starting transfers between devices: 8.05 us -> 0 us
  local copies, waits for them, and re-layouts: 15 us -> 7.35 us
  other arithmetic: 4.79 us -> 0 us
    psum x1 -> x0, blocking collectives: 123 us -> none  [per_device(): totals = lax.psum((weighted, area_total), ('region', 'tile'))]
    all_gather x1 -> x0, blocking collectives: 61 us -> none  [per_device(): sources = lax.all_gather(send_src, 'tile', axis=0, tiled=True)]
    pallas_call x0 -> x1, Pallas kernels: none -> 58 us  [per_device(): pl.pallas_call(functools.partial(kernel, regions, tiles), out_shape=(jax....]
    all_gather x1 -> x0, waiting for transfers between devices: 40.2 us -> none  [per_device(): piece = lax.all_gather(atm_state, 'tile', axis=0, tiled=True)]
    dot_general x5 -> x0, matrix products: 12.1 us -> none  [the longest x1 3.15 us: per_device(): jnp.einsum('scb,sbo->sco', fetched.reshape(slot_count, channels, columns)...]
    all_to_all x1 -> x0, waiting for transfers between devices: 9.42 us -> none  [per_device(): lax.all_to_all(back.reshape(tile_count, slot_depth, flux_fields * columns...]
    all_to_all x1 -> x0, starting transfers between devices: 8.01 us -> none  [per_device(): lax.all_to_all(back.reshape(tile_count, slot_depth, flux_fields * columns...]
    unnamed x15 -> x16, local copies, waits for them, and re-layouts: 0.91 us -> 7.35 us
  transfers between devices with their start and end apart: 2 -> 0, of which waited for: 2 -> 0; matrix products, arithmetic and copies ran while one was open for 2% -> 0% of each run, Pallas kernels for 0% -> 0%
where the time goes in v1:
time: 66.4 us; the launch traced here: 66 us
  Pallas kernels  58 us (87%)
  local copies, waits for them, and re-layouts  7.35 us (11%)
    pallas_call x1, Pallas kernels, per_device(): pl.pallas_call(functools.partial(kernel, regions, tiles), out_shape=(jax....  58 us
    unnamed x16, local copies, waits for them, and re-layouts  7.35 us

profile of v1, /device:TPU:1, one launch (start us, length us, event | category | flops | bytes accessed | tf_op | source)
XLA Modules:
  0.0 66.0 jit_solution(15040719079584932594)
XLA Ops:
  0.6 0.0 copy-start
  0.6 1.6 %copy-done = bf16[256,32,128]{2,1,0:T(8,128)(2,1)S(1)} copy-done((bf16[256,32,128]{2,1,0:T(8,128)(2,1)S(1)}, bf16[256,32,128]{2,1,0:T(8,128)(2,1)}, u32[]{:S(2)}) %copy-start) | copy-done | bytes 2097176
  2.2 0.0 copy-start.1
  2.2 0.9 %copy-done.1 = f32[64,512]{1,0:T(8,128)S(1)} copy-done((f32[64,512]{1,0:T(8,128)S(1)}, f32[64,512]{1,0:T(8,128)}, u32[]{:S(2)}) %copy-start.1) | copy-done | bytes 131096
  3.1 0.0 copy-start.2
  3.1 0.8 %copy-done.2 = bf16[16,1280]{1,0:T(8,128)(2,1)S(1)} copy-done((bf16[16,1280]{1,0:T(8,128)(2,1)S(1)}, bf16[16,1280]{1,0:T(8,128)(2,1)}, u32[]{:S(2)}) %copy-start.2) | copy-done | bytes 40984
  3.9 0.0 copy-start.3
  3.9 0.8 %copy-done.3 = f32[64,128]{1,0:T(8,128)S(1)} copy-done((f32[64,128]{1,0:T(8,128)S(1)}, f32[64,128]{1,0:T(8,128)}, u32[]{:S(2)}) %copy-start.3) | copy-done | bytes 32792
  4.7 0.0 copy-start.4
  4.7 0.7 %copy-done.4 = s32[1,64,4]{1,2,0:T(4,128)S(1)} copy-done((s32[1,64,4]{1,2,0:T(4,128)S(1)}, s32[1,64,4]{1,2,0:T(4,128)}, u32[]{:S(2)}) %copy-start.4) | copy-done | bytes 1048
  5.3 0.0 copy-start.5
  5.4 0.7 %copy-done.5 = s32[1,64,4]{1,2,0:T(4,128)S(1)} copy-done((s32[1,64,4]{1,2,0:T(4,128)S(1)}, s32[1,64,4]{1,2,0:T(4,128)}, u32[]{:S(2)}) %copy-start.5) | copy-done | bytes 1048
  6.0 0.0 copy-start.6
  6.0 0.7 copy-done.6
  6.7 58.0 %couple.1 = (f32[64,1024]{1,0:T(8,128)S(1)}, f32[16,256]{1,0:T(8,128)S(1)}) custom-call(bf16[16,1280]{1,0:T(8,128)(2,1)S(1)} %copy-done.2, f32[64,512]{1,0:T(8,128)S(1)} %copy-done.1, f32[64,128]{1,0:T(8,128)S(1)} %copy-done.3, f32[4]{0:T(128)S(1)} %copy-done.6, bf16[8192,128]{1,0:T(8,128)(2,1)S(1)} %bitcast.3, s32[1,4,64]{2,1,0:T(4,128)S(1)} %bitcast.4, ...), custom_call_target="tpu_custom_call" | custom-call | flops 400000000 | bytes 4000000 | tf_op jit(solution)/shard_map/couple/pallas_call | solution.py:286
  64.7 0.7 %copy.11 = f32[64,1024]{1,0:T(8,128)} copy(f32[64,1024]{1,0:T(8,128)S(1)} %get-tuple-element.4) | data formatting | bytes 524288
  65.4 0.6 copy.12
Async XLA Ops:
  0.6 1.6 %copy-start = (bf16[256,32,128]{2,1,0:T(8,128)(2,1)S(1)}, bf16[256,32,128]{2,1,0:T(8,128)(2,1)}, u32[]{:S(2)}) copy-start(bf16[256,32,128]{2,1,0:T(8,128)(2,1)} %param.11) | copy-start | bytes 6291460
  2.2 0.9 %copy-start.1 = (f32[64,512]{1,0:T(8,128)S(1)}, f32[64,512]{1,0:T(8,128)}, u32[]{:S(2)}) copy-start(f32[64,512]{1,0:T(8,128)} %ocean_ref.1) | copy-start | bytes 393220
  3.1 0.8 %copy-start.2 = (bf16[16,1280]{1,0:T(8,128)(2,1)S(1)}, bf16[16,1280]{1,0:T(8,128)(2,1)}, u32[]{:S(2)}) copy-start(bf16[16,1280]{1,0:T(8,128)(2,1)} %atm_ref.1) | copy-start | bytes 122884
  3.9 0.8 %copy-start.3 = (f32[64,128]{1,0:T(8,128)S(1)}, f32[64,128]{1,0:T(8,128)}, u32[]{:S(2)}) copy-start(f32[64,128]{1,0:T(8,128)} %area_ref.1) | copy-start | bytes 98308
  4.7 0.7 %copy-start.4 = (s32[1,64,4]{1,2,0:T(4,128)S(1)}, s32[1,64,4]{1,2,0:T(4,128)}, u32[]{:S(2)}) copy-start(s32[1,64,4]{1,2,0:T(4,128)} %param.12) | copy-start | bytes 3076
  5.3 0.7 %copy-start.5 = (s32[1,64,4]{1,2,0:T(4,128)S(1)}, s32[1,64,4]{1,2,0:T(4,128)}, u32[]{:S(2)}) copy-start(s32[1,64,4]{1,2,0:T(4,128)} %param.13) | copy-start | bytes 3076
  6.0 0.7 copy-start.6

commit v2 on v1

v2 whole, which is shorter than its diff:
```python
import functools

import jax
import jax.numpy as jnp
from jax import lax
from jax.experimental import pallas as pl
from jax.experimental.pallas import tpu as pltpu
from jax.sharding import PartitionSpec as P

F32 = jnp.float32
BF16 = jnp.bfloat16
MESH = pl.DeviceIdType.MESH
CLASSES = 4
FORWARD_UNROLL = 4
BACK_STEP = 4


def iota(shape, axis):
    return lax.broadcasted_iota(jnp.int32, shape, axis)


def two_parts(x):
    high = x.astype(BF16)
    return high, (x - high.astype(F32)).astype(BF16)


def dot(a, b, contract=((1,), (0,))):
    return lax.dot_general(a, b, (contract, ((), ())), preferred_element_type=F32)


def softplus(x):
    return jnp.maximum(x, 0.0) + jnp.log1p(jnp.exp(-jnp.abs(x)))


def fluxes(bottom, surface):
    sst, ocean_u, ocean_v, albedo_in = surface
    wind_x = bottom[0] - ocean_u
    wind_y = bottom[1] - ocean_v
    speed = jnp.sqrt(wind_x * wind_x + wind_y * wind_y + bottom[9] * bottom[9] + 1.0)
    transfer = 0.1 * jnp.exp(0.2 * jnp.tanh(bottom[8])) * speed
    stress_x = transfer * wind_x
    stress_y = transfer * wind_y
    sensible = transfer * (bottom[2] - sst)
    saturated = jnp.exp(0.1 * sst - 0.1 * jnp.tanh(bottom[7]))
    latent = transfer * (bottom[3] - saturated)
    albedo = 0.05 + 0.3 * (1.0 / (1.0 + jnp.exp(-albedo_in)))
    shortwave = (1.0 - albedo) * softplus(bottom[4])
    longwave = softplus(bottom[5]) - 1.0 - 0.2 * sst
    freshwater = softplus(bottom[6]) + latent
    heating = sensible + latent + shortwave + longwave
    return [stress_x, stress_y, sensible, latent, shortwave, longwave, freshwater, heating]


def chip_grid(tiles):
    chips = tiles // 2
    height = min(8, chips)
    return chips // height, height


def outward(k, size):
    step = (k + 1) // 2
    return size // 2 + step * (1 - 2 * (k % 2))


def kernel(
    regions, tiles, atm_hbm, ocean_hbm, area_hbm, weights_ref, remap_hbm, src_hbm, owner_hbm,
    ocean_out, atm_out,
    atm_ref, ocean_ref, area_ref, src_ref, owner_ref,
    remap, send1, recv1, contrib, rows_back, send2, recv2, trows, zrows,
    load_sem, send1_sem, recv1_sem, send2_sem, recv2_sem, tsend_sem, trecv_sem, zsend_sem, zrecv_sem,
):
    region = lax.axis_index("region")
    tile = lax.axis_index("tile")
    cap = src_ref.shape[1]
    atm_blocks = atm_ref.shape[0]
    ocean_blocks, cells = area_ref.shape
    nf = atm_ref.shape[1] // cells
    columns = cells // cap
    slots = tiles * cap
    nflx = 8
    wide, high_grid = chip_grid(tiles)
    chips = tiles // 2
    per_class = chips // CLASSES
    depth = 8 * columns

    loads = [
        pltpu.make_async_copy(source, target, load_sem.at[n])
        for n, (source, target) in enumerate(
            [
                (atm_hbm, atm_ref),
                (src_hbm, src_ref),
                (owner_hbm, owner_ref),
                (ocean_hbm, ocean_ref),
                (area_hbm, area_ref),
                (remap_hbm, remap),
            ]
        )
    ]

    barrier = pltpu.get_barrier_semaphore()
    my_chip = tile // 2
    core = tile % 2

    def chip_at(k, sign):
        away_y = outward(k // wide, high_grid)
        away_x = outward(k % wide, wide)
        x = (my_chip // high_grid + sign * away_x + wide) % wide
        y = (my_chip % high_grid + sign * away_y + high_grid) % high_grid
        return x * high_grid + y

    def peers(visit):
        for n in range(CLASSES):

            @pl.loop(n * per_class, min((n + 1) * per_class, chips - 1))
            def _(k):
                chip = chip_at(k, 1)
                visit(n, chip * 2 + core)
                visit(n, chip * 2 + 1 - core)

        visit(CLASSES - 1, my_chip * 2 + 1 - core)

    @pl.loop(1, regions)
    def _(i):
        peer = (region + i) % regions
        pl.semaphore_signal(barrier, inc=1, device_id=(peer, tile), device_id_type=MESH)

    def greet(_, peer):
        pl.semaphore_signal(barrier, inc=1, device_id=(region, peer), device_id_type=MESH)

    peers(greet)
    for load in loads:
        load.start()
    for load in loads[:3]:
        load.wait()

    lane = iota((atm_blocks, cells), 1)
    level = lane // columns
    level_weight = jnp.zeros((atm_blocks, cells), F32)
    for l in range(cap):
        level_weight = jnp.where(level == l, weights_ref[l], level_weight)
    pieces = []
    for f in range(nf):
        x = atm_ref[:, f * cells : (f + 1) * cells].astype(F32) * level_weight
        x = x + pltpu.roll(x, 2 * columns, 1)
        pieces.append(x + pltpu.roll(x, columns, 1))
    combined = jnp.concatenate(pieces, axis=1)
    block = iota((atm_blocks, nf * cells), 1) % cells // columns
    stacked = jnp.concatenate([jnp.where(block == c, combined, 0.0) for c in range(cap)], axis=0)
    first, second = two_parts(stacked)
    third = (stacked - first.astype(F32) - second.astype(F32)).astype(BF16)
    table = jnp.concatenate([first, second, third], axis=0)
    width = 3 * cap * atm_blocks
    at = iota((width, tiles), 0)
    wanted = jnp.full((width, tiles), -1, jnp.int32)
    for c in range(cap):
        wanted = jnp.where(at // atm_blocks % cap == c, src_ref[0, c : c + 1, :], wanted)
    pick = jnp.where(wanted == at % atm_blocks, 1.0, 0.0).astype(BF16)
    packed = dot(pick, table, ((0,), (0,)))
    for f in range(nf):
        send1[:, f, :] = packed[:, f * cells : (f + 1) * cells]

    at = iota((tiles, slots), 1)
    repeat = jnp.where(at // 8 * 2 + at % 2 == iota((tiles, slots), 0), 1.0, 0.0)
    by_slot = dot(owner_ref[0].astype(F32).astype(BF16), repeat.astype(BF16))
    own_row = iota((cap, slots), 0) == iota((cap, slots), 1) % 8 // 2
    owner_of = jnp.sum(jnp.where(own_row, by_slot, 0.0), axis=0, keepdims=True)
    feeds = jnp.where(
        owner_of.astype(jnp.int32) == iota((ocean_blocks, slots), 0), 1.0, 0.0
    ).astype(BF16)

    recv1[pl.ds(tile, 1), pl.ds(0, nf), :] = send1[pl.ds(tile, 1), pl.ds(0, nf), :]

    pl.semaphore_wait(barrier, tiles - 1 + regions - 1)

    def send(source, target, rows, send_sem, recv_sem, peer):
        pltpu.make_async_remote_copy(
            src_ref=source.at[peer, pl.ds(0, rows)],
            dst_ref=target.at[tile, pl.ds(0, rows)],
            send_sem=send_sem,
            recv_sem=recv_sem,
            device_id=(region, peer),
            device_id_type=MESH,
        ).start()

    def drain(buffer, count, rows, sem):
        whole = buffer.at[pl.ds(0, count), pl.ds(0, rows)]
        pltpu.make_async_copy(whole, whole, sem).wait()

    peers(lambda n, peer: send(send1, recv1, nf, send1_sem, recv1_sem.at[n], peer))

    for load in loads[3:]:
        load.wait()

    row8 = iota((8, cells), 0)
    lane8 = iota((8, cells), 1)
    own_lanes = row8 // 2 == lane8 // columns
    even = row8 % 2 == 0
    diagonal = [own_lanes & even, own_lanes & (row8 % 2 == 1)]

    def group(g):
        return remap[pl.ds(pl.multiple_of(g * depth, depth), depth), :]

    def forward(k):
        g = chip_at(k, -1)
        halves = []
        for h in range(2):
            rows = [
                jnp.where(
                    diagonal[h],
                    jnp.broadcast_to(recv1[g * 2 + h, pl.ds(f, 1), :], (8, cells)),
                    0.0,
                )
                for f in range(nf)
            ]
            halves.append(jnp.concatenate(rows, axis=0))
        high, low = two_parts(jnp.concatenate(halves, axis=1))
        w = group(g)
        out = dot(high, w) + dot(low, w)
        for f in range(nf):
            contrib[pl.ds(pl.multiple_of(g * 8, 8), 8), f * cells : (f + 1) * cells] = out[
                f * 8 : (f + 1) * 8
            ]

    for n in range(CLASSES):
        arriving = 2 * per_class - (n == CLASSES - 1)
        drain(recv1, arriving, nf, recv1_sem.at[n])

        @pl.loop(n * per_class, (n + 1) * per_class, unroll=min(FORWARD_UNROLL, per_class))
        def _(k):
            forward(k)

    high, low = two_parts(contrib[...])
    bottom = dot(feeds, high) + dot(feeds, low)
    raw = fluxes(
        [bottom[:, f * cells : (f + 1) * cells] for f in range(nf)],
        [ocean_ref[:, f * cells : (f + 1) * cells] for f in range(4)],
    )
    fresh = raw[6]

    weighted = jnp.sum(area_ref[...] * fresh, axis=0, keepdims=True)
    total = jnp.sum(area_ref[...], axis=0, keepdims=True)
    half = cells // 2
    low_lanes = iota((1, cells), 1) < half
    sums = jnp.where(
        low_lanes, weighted + pltpu.roll(weighted, half, 1), total + pltpu.roll(total, half, 1)
    )
    trows[pl.ds(tile, 1), pl.ds(0, 1), :] = sums.reshape(1, 1, cells)

    def send_sums(_, peer):
        pltpu.make_async_remote_copy(
            src_ref=trows.at[tile, pl.ds(0, 1)],
            dst_ref=trows.at[tile, pl.ds(0, 1)],
            send_sem=tsend_sem,
            recv_sem=trecv_sem,
            device_id=(region, peer),
            device_id_type=MESH,
        ).start()

    peers(send_sums)

    for f in range(nflx):
        if f != 6:
            ocean_out[:, f * cells : (f + 1) * cells] = raw[f]
    fresh_high, fresh_low = two_parts(fresh)
    fields = [r.astype(BF16) for r in raw]
    fields[6] = fresh_high
    rows_back[...] = dot(feeds, jnp.concatenate(fields + [fresh_low], axis=1), ((0,), (0,)))
    ones = jnp.ones((8, cells), F32)

    def pair(a, b):
        upper = row8 < 4
        return jnp.where(upper, a, b) + pltpu.roll(jnp.where(upper, b, a), 4, 0)

    def four(a, b):
        near = row8 % 4 < 2
        x = jnp.where(near, b, a)
        return jnp.where(near, a, b) + jnp.where(near, pltpu.roll(x, 6, 0), pltpu.roll(x, 2, 0))

    def backward(g):
        at_rows = pl.ds(pl.multiple_of(g * 8, 8), 8)
        rows = [rows_back[at_rows, f * cells : (f + 1) * cells] for f in range(nflx + 1)]
        left = jnp.concatenate(rows + [ones], axis=0).astype(BF16)
        out = dot(left, group(g), ((1,), (1,)))
        x = []
        for f in range(nflx + 1):
            piece = out[f * 8 : (f + 1) * 8]
            mixed = jnp.where(even, piece[:, :cells], piece[:, cells:])
            x.append(jnp.where(own_lanes, mixed, 0.0))
        x[6] = x[6] + x[nflx]
        q0 = four(pair(x[0], x[4]), pair(x[2], x[6]))
        q1 = four(pair(x[1], x[5]), pair(x[3], x[7]))
        send2[g * 2, pl.ds(0, 8), :] = jnp.where(even, q0, pltpu.roll(q1, 1, 0))
        send2[g * 2 + 1, pl.ds(0, 8), :] = jnp.where(even, pltpu.roll(q0, 7, 0), q1)
        for h in range(2):
            at = (nflx + 1) * 8
            send2[g * 2 + h, pl.ds(nflx, 1), :] = out[at : at + 1, h * cells : (h + 1) * cells]

    @pl.loop(0, (chips - 1) // BACK_STEP)
    def _(i):
        for u in range(BACK_STEP):
            backward(chip_at(i * BACK_STEP + u, 1))
        for u in range(BACK_STEP):
            chip = chip_at(i * BACK_STEP + u, 1)
            for peer in (chip * 2 + core, chip * 2 + 1 - core):
                send(send2, recv2, nflx + 1, send2_sem, recv2_sem, peer)

    for k in range((chips - 1) // BACK_STEP * BACK_STEP, chips - 1):
        backward(chip_at(k, 1))
        for peer in (chip_at(k, 1) * 2 + core, chip_at(k, 1) * 2 + 1 - core):
            send(send2, recv2, nflx + 1, send2_sem, recv2_sem, peer)
    backward(my_chip)
    send(send2, recv2, nflx + 1, send2_sem, recv2_sem, my_chip * 2 + 1 - core)
    recv2[pl.ds(tile, 1), pl.ds(0, nflx + 1), :] = send2[pl.ds(tile, 1), pl.ds(0, nflx + 1), :]

    drain(trows, tiles - 1, 1, trecv_sem)
    sums = jnp.sum(trows[:, 0, :], axis=0, keepdims=True)
    zrows[pl.ds(region, 1), pl.ds(0, 1), :] = sums.reshape(1, 1, cells)

    @pl.loop(1, regions)
    def _(i):
        peer = (region + i) % regions
        pltpu.make_async_remote_copy(
            src_ref=zrows.at[region, pl.ds(0, 1)],
            dst_ref=zrows.at[region, pl.ds(0, 1)],
            send_sem=zsend_sem,
            recv_sem=zrecv_sem,
            device_id=(peer, tile),
            device_id_type=MESH,
        ).start()

    drain(recv2, tiles - 1, nflx + 1, recv2_sem)
    if regions > 1:
        drain(zrows, regions - 1, 1, zrecv_sem)
    sums_all = jnp.sum(zrows[:, 0, :], axis=0, keepdims=True)
    weighted_all = jnp.sum(jnp.where(low_lanes, sums_all, 0.0), axis=1, keepdims=True)
    area_all = jnp.sum(jnp.where(low_lanes, 0.0, sums_all), axis=1, keepdims=True)
    shift = weighted_all / area_all
    ocean_out[:, 6 * cells : 7 * cells] = fresh - shift

    back = []
    for f in range(nflx):
        x = recv2[:, f, :]
        if f == 6:
            x = x - shift * recv2[:, nflx, :]
        back.append(x.astype(BF16))
    gathered = dot(pick[: cap * atm_blocks], jnp.concatenate(back, axis=1))
    lane_group = iota((atm_blocks, cells), 1) // columns
    outs = []
    for f in range(nflx):
        x = jnp.zeros((atm_blocks, cells), F32)
        for c in range(cap):
            x = jnp.where(
                lane_group == c,
                gathered[c * atm_blocks : (c + 1) * atm_blocks, f * cells : (f + 1) * cells],
                x,
            )
        x = x + pltpu.roll(x, 2 * columns, 1)
        outs.append(x + pltpu.roll(x, columns, 1))
    for t in range(nflx // cap):
        x = outs[t * cap]
        for c in range(1, cap):
            x = jnp.where(lane_group == c, outs[t * cap + c], x)
        atm_out[:, t * cells : (t + 1) * cells] = x

    drain(send1, tiles - 1, nf, send1_sem)
    drain(send2, tiles - 1, nflx + 1, send2_sem)
    drain(trows, tiles - 1, 1, tsend_sem)
    if regions > 1:
        drain(zrows, regions - 1, 1, zsend_sem)


def per_device(
    regions, tiles, atm_state, ocean_state, cell_area, level_weights, remap, send_src, recv_ocn
):
    cap = send_src.shape[2]
    slots = tiles * cap
    atm_blocks = atm_state.shape[0]
    ocean_blocks, cells = cell_area.shape
    columns = remap.shape[1]
    nf = atm_state.shape[1] // cells
    nflx = 8
    vmem = pl.BlockSpec(memory_space=pltpu.VMEM)
    hbm = pl.BlockSpec(memory_space=pltpu.HBM)
    box = pltpu.VMEM((tiles, 16, cells), F32)
    dma = pltpu.SemaphoreType.DMA
    return pl.pallas_call(
        functools.partial(kernel, regions, tiles),
        out_shape=(
            jax.ShapeDtypeStruct((ocean_blocks, nflx * cells), F32),
            jax.ShapeDtypeStruct((atm_blocks, nflx * columns), F32),
        ),
        in_specs=[hbm, hbm, hbm, pl.BlockSpec(memory_space=pltpu.SMEM), hbm, hbm, hbm],
        out_specs=(vmem, vmem),
        scratch_shapes=[
            pltpu.VMEM(atm_state.shape, BF16),
            pltpu.VMEM(ocean_state.shape, F32),
            pltpu.VMEM(cell_area.shape, F32),
            pltpu.VMEM((1, cap, tiles), jnp.int32),
            pltpu.VMEM((1, cap, tiles), jnp.int32),
            pltpu.VMEM((slots * columns, cells), BF16),
            box,
            box,
            pltpu.VMEM((slots, nf * cells), F32),
            pltpu.VMEM((slots, (nflx + 1) * cells), F32),
            box,
            box,
            pltpu.VMEM((tiles, 8, cells), F32),
            pltpu.VMEM((regions, 8, cells), F32),
            pltpu.SemaphoreType.DMA((6,)),
            dma,
            pltpu.SemaphoreType.DMA((CLASSES,)),
            dma, dma, dma, dma, dma, dma,
        ],
        compiler_params=pltpu.CompilerParams(
            collective_id=0, has_side_effects=True, vmem_limit_bytes=60 * 1024 * 1024
        ),
        cost_estimate=pl.CostEstimate(
            flops=400_000_000, bytes_accessed=4_000_000, transcendentals=100_000
        ),
        name="couple",
    )(
        atm_state, ocean_state, cell_area, level_weights,
        remap.reshape(slots * columns, cells),
        jnp.swapaxes(send_src, 1, 2), jnp.swapaxes(recv_ocn, 1, 2),
    )


def solution(mesh):
    in_specs = (
        P(("region", "tile"), None),
        P(("region", "tile"), None),
        P(("region", "tile"), None),
        P(),
        P(("region", "tile"), None, None),
        P(("region", "tile"), None, None),
        P(("region", "tile"), None, None),
    )
    out_specs = (P(("region", "tile"), None), P(("region", "tile"), None))
    return jax.shard_map(
        functools.partial(per_device, mesh.shape["region"], mesh.shape["tile"]),
        mesh=mesh,
        in_specs=in_specs,
        out_specs=out_specs,
        check_vma=False,
    )
```

time: 66.4 us -> 53.9 us (0.81)
  Pallas kernels: 58 us -> 50 us
  local copies, waits for them, and re-layouts: 7.35 us -> 2.99 us
    pallas_call x1, Pallas kernels: 58 us -> 50 us  [per_device(): pl.pallas_call(functools.partial(kernel, regions, tiles), out_shape=(jax....]
    unnamed x16 -> x2, local copies, waits for them, and re-layouts: 7.35 us -> 2.99 us
where the time goes in v2:
time: 53.9 us; the launch traced here: 53.6 us
  Pallas kernels  50 us (93%)
  local copies, waits for them, and re-layouts  2.99 us (6%)
  between operations  0.64 us (1%)
    pallas_call x1, Pallas kernels, per_device(): pl.pallas_call(functools.partial(kernel, regions, tiles), out_shape=(jax....  50 us
    unnamed x2, local copies, waits for them, and re-layouts  2.99 us

profile of v2, /device:TPU:1, one launch (start us, length us, event | category | flops | bytes accessed | tf_op | source)
XLA Modules:
  0.0 53.6 jit_solution(12011448543645753578)
XLA Ops:
  0.6 50.0 %couple.1 = (f32[64,1024]{1,0:T(8,128)}, f32[16,256]{1,0:T(8,128)}) custom-call(bf16[16,1280]{1,0:T(8,128)(2,1)} %atm_hbm.1, f32[64,512]{1,0:T(8,128)} %ocean_hbm.1, f32[64,128]{1,0:T(8,128)} %area_hbm.1, f32[4]{0:T(128)} %weights_ref.1, bf16[8192,128]{1,0:T(8,128)(2,1)} %bitcast.3, s32[1,4,64]{2,1,0:T(4,128)} %bitcast.4, s32[1,4,64]{2,1,0:T(4,128)} %bitcast.5), custom_call_target="tpu_custom_call" | custom-call | flops 400000000 | bytes 4000000 | tf_op jit(solution)/shard_map/couple/pallas_call | solution.py:386
  50.6 1.7 %copy.11 = f32[64,1024]{1,0:T(8,128)} copy(f32[64,1024]{1,0:T(8,128)} %get-tuple-element.4) | data formatting | bytes 524288
  52.3 1.3 %copy.12 = f32[16,256]{1,0:T(8,128)} copy(f32[16,256]{1,0:T(8,128)} %get-tuple-element.5) | data formatting | bytes 32768

commit v3 on v2

v3 whole, which is shorter than its diff:
```python
import functools

import jax
import jax.numpy as jnp
from jax import lax
from jax.experimental import pallas as pl
from jax.experimental.pallas import tpu as pltpu
from jax.sharding import PartitionSpec as P

F32 = jnp.float32
BF16 = jnp.bfloat16
MESH = pl.DeviceIdType.MESH
CLASSES = 4
FORWARD_UNROLL = 4
BACK_STEP = 4
ROOTS = 2
EARLY = (0, 1, 3, 6, 7, 8, 9)
LATE = (2, 4, 5)
LATE_ROW = 8


def iota(shape, axis):
    return lax.broadcasted_iota(jnp.int32, shape, axis)


def two_parts(x):
    high = x.astype(BF16)
    return high, (x - high.astype(F32)).astype(BF16)


def dot(a, b, contract=((1,), (0,))):
    return lax.dot_general(a, b, (contract, ((), ())), preferred_element_type=F32)


def softplus(x):
    return jnp.maximum(x, 0.0) + jnp.log1p(jnp.exp(-jnp.abs(x)))


def freshwater_flux(bottom, surface):
    sst, ocean_u, ocean_v, _ = surface
    wind_x = bottom[0] - ocean_u
    wind_y = bottom[1] - ocean_v
    speed = jnp.sqrt(wind_x * wind_x + wind_y * wind_y + bottom[9] * bottom[9] + 1.0)
    transfer = 0.1 * jnp.exp(0.2 * jnp.tanh(bottom[8])) * speed
    saturated = jnp.exp(0.1 * sst - 0.1 * jnp.tanh(bottom[7]))
    latent = transfer * (bottom[3] - saturated)
    return transfer, latent, softplus(bottom[6]) + latent


def fluxes(bottom, surface, transfer, latent, freshwater):
    sst, ocean_u, ocean_v, albedo_in = surface
    stress_x = transfer * (bottom[0] - ocean_u)
    stress_y = transfer * (bottom[1] - ocean_v)
    sensible = transfer * (bottom[2] - sst)
    albedo = 0.05 + 0.3 * (1.0 / (1.0 + jnp.exp(-albedo_in)))
    shortwave = (1.0 - albedo) * softplus(bottom[4])
    longwave = softplus(bottom[5]) - 1.0 - 0.2 * sst
    heating = sensible + latent + shortwave + longwave
    return [stress_x, stress_y, sensible, latent, shortwave, longwave, freshwater, heating]


def chip_grid(tiles):
    chips = tiles // 2
    height = min(8, chips)
    return chips // height, height


def outward(k, size):
    step = (k + 1) // 2
    return size // 2 + step * (1 - 2 * (k % 2))


def kernel(
    regions, tiles, atm_hbm, ocean_hbm, area_hbm, weights_ref, remap_hbm, src_hbm, owner_hbm,
    ocean_hbm_out, atm_hbm_out,
    atm_ref, ocean_ref, area_ref, src_ref, owner_ref, ocean_out, atm_out,
    remap, send1, recv1, contrib, total_ref, rows_back, send2, recv2, trows, zrows, zmean,
    load_sem, send1_sem, recv1_sem, send2_sem, recv2_sem, tsend_sem, trecv_sem, zsend_sem, zrecv_sem,
    msend_sem, mrecv_sem, late_send_sem, late_recv_sem, out_sem,
):
    region = lax.axis_index("region")
    tile = lax.axis_index("tile")
    cap = src_ref.shape[1]
    atm_blocks = atm_ref.shape[0]
    ocean_blocks, cells = area_ref.shape
    nf = atm_ref.shape[1] // cells
    columns = cells // cap
    slots = tiles * cap
    nflx = 8
    wide, high_grid = chip_grid(tiles)
    chips = tiles // 2
    per_class = chips // CLASSES
    depth = 8 * columns

    loads = [
        pltpu.make_async_copy(source, target, load_sem.at[n])
        for n, (source, target) in enumerate(
            [
                (atm_hbm, atm_ref),
                (src_hbm, src_ref),
                (owner_hbm, owner_ref),
                (ocean_hbm, ocean_ref),
                (area_hbm, area_ref),
                (remap_hbm, remap),
            ]
        )
    ]

    barrier = pltpu.get_barrier_semaphore()
    my_chip = tile // 2
    core = tile % 2

    def chip_at(k, sign):
        away_y = outward(k // wide, high_grid)
        away_x = outward(k % wide, wide)
        x = (my_chip // high_grid + sign * away_x + wide) % wide
        y = (my_chip % high_grid + sign * away_y + high_grid) % high_grid
        return x * high_grid + y

    def peers(visit):
        for n in range(CLASSES):

            @pl.loop(n * per_class, min((n + 1) * per_class, chips - 1))
            def _(k):
                chip = chip_at(k, 1)
                visit(n, chip * 2 + core)
                visit(n, chip * 2 + 1 - core)

        visit(CLASSES - 1, my_chip * 2 + 1 - core)

    roots = min(ROOTS, regions)
    near, stride = max(regions // 2, roots), regions // 4
    is_root = region < roots
    hands_on = (region >= near - stride) & (region < regions - stride) & (near < regions)
    greeted = jnp.where(is_root, regions - 1, 1)
    reached = jnp.where(
        region == 0, near - 1, jnp.where(is_root, roots - 1, roots)
    ) + hands_on.astype(jnp.int32)

    if regions > 1:

        @pl.loop(0, greeted)
        def _(i):
            apart = (region + outward(i, regions) + regions) % regions
            giver = jnp.where(region < near, 0, region - stride)
            peer = jnp.where(is_root, apart, giver)
            pl.semaphore_signal(barrier, inc=1, device_id=(peer, tile), device_id_type=MESH)

    def greet(_, peer):
        pl.semaphore_signal(barrier, inc=1, device_id=(region, peer), device_id_type=MESH)

    peers(greet)
    for load in loads:
        load.start()
    for load in loads[:3]:
        load.wait()

    lane = iota((atm_blocks, cells), 1)
    level = lane // columns
    level_weight = jnp.zeros((atm_blocks, cells), F32)
    for l in range(cap):
        level_weight = jnp.where(level == l, weights_ref[l], level_weight)
    pieces = []
    for f in range(nf):
        x = atm_ref[:, f * cells : (f + 1) * cells].astype(F32) * level_weight
        x = x + pltpu.roll(x, 2 * columns, 1)
        pieces.append(x + pltpu.roll(x, columns, 1))
    combined = jnp.concatenate(pieces, axis=1)
    block = iota((atm_blocks, nf * cells), 1) % cells // columns
    stacked = jnp.concatenate([jnp.where(block == c, combined, 0.0) for c in range(cap)], axis=0)
    first, second = two_parts(stacked)
    third = (stacked - first.astype(F32) - second.astype(F32)).astype(BF16)
    table = jnp.concatenate([first, second, third], axis=0)
    width = 3 * cap * atm_blocks
    at = iota((width, tiles), 0)
    wanted = jnp.full((width, tiles), -1, jnp.int32)
    for c in range(cap):
        wanted = jnp.where(at // atm_blocks % cap == c, src_ref[0, c : c + 1, :], wanted)
    pick = jnp.where(wanted == at % atm_blocks, 1.0, 0.0).astype(BF16)
    packed = dot(pick, table, ((0,), (0,)))
    early, late = len(EARLY), len(LATE)
    early_rows, late_rows = (0, early), (LATE_ROW, late)
    for start, fields in ((0, EARLY), (LATE_ROW, LATE)):
        for n, f in enumerate(fields):
            send1[:, start + n, :] = packed[:, f * cells : (f + 1) * cells]

    at = iota((tiles, slots), 1)
    sender = chip_at(at // 8, -1) * 2 + at % 2
    repeat = jnp.where(sender == iota((tiles, slots), 0), 1.0, 0.0)
    by_slot = dot(owner_ref[0].astype(F32).astype(BF16), repeat.astype(BF16))
    own_row = iota((cap, slots), 0) == iota((cap, slots), 1) % 8 // 2
    owner_of = jnp.sum(jnp.where(own_row, by_slot, 0.0), axis=0, keepdims=True)
    feeds = jnp.where(
        owner_of.astype(jnp.int32) == iota((ocean_blocks, slots), 0), 1.0, 0.0
    ).astype(BF16)

    for rows in (early_rows, late_rows):
        recv1[pl.ds(tile, 1), pl.ds(*rows), :] = send1[pl.ds(tile, 1), pl.ds(*rows), :]

    pl.semaphore_wait(barrier, tiles - 1 + (reached if regions > 1 else 0))

    def send(source, target, rows, send_sem, recv_sem, peer):
        pltpu.make_async_remote_copy(
            src_ref=source.at[peer, pl.ds(*rows)],
            dst_ref=target.at[tile, pl.ds(*rows)],
            send_sem=send_sem,
            recv_sem=recv_sem,
            device_id=(region, peer),
            device_id_type=MESH,
        ).start()

    def drain(buffer, count, rows, sem):
        whole = buffer.at[pl.ds(0, count), pl.ds(0, rows)]
        pltpu.make_async_copy(whole, whole, sem).wait()

    peers(lambda n, peer: send(send1, recv1, early_rows, send1_sem, recv1_sem.at[n], peer))
    peers(lambda n, peer: send(send1, recv1, late_rows, late_send_sem, late_recv_sem, peer))

    for load in loads[3:]:
        load.wait()

    row8 = iota((8, cells), 0)
    lane8 = iota((8, cells), 1)
    own_lanes = row8 // 2 == lane8 // columns
    even = row8 % 2 == 0
    diagonal = [own_lanes & even, own_lanes & (row8 % 2 == 1)]

    def group(g):
        return remap[pl.ds(pl.multiple_of(g * depth, depth), depth), :]

    def forward(k, start, rows_in, column):
        g = chip_at(k, -1)
        halves = []
        for h in range(2):
            rows = [
                jnp.where(
                    diagonal[h],
                    jnp.broadcast_to(recv1[g * 2 + h, pl.ds(start + f, 1), :], (8, cells)),
                    0.0,
                )
                for f in range(rows_in)
            ]
            halves.append(jnp.concatenate(rows, axis=0))
        high, low = two_parts(jnp.concatenate(halves, axis=1))
        w = group(g)
        out = dot(high, w) + dot(low, w)
        for f in range(rows_in):
            at = (column + f) * cells
            contrib[pl.ds(pl.multiple_of(k * 8, 8), 8), at : at + cells] = out[
                f * 8 : (f + 1) * 8
            ]

    def select(some, columns_in):
        high, low = two_parts(contrib[some, columns_in])
        return dot(feeds[:, some], high) + dot(feeds[:, some], low)

    early_columns, late_columns = slice(0, early * cells), slice(early * cells, nf * cells)
    for n in range(CLASSES):
        drain(recv1, 2 * per_class - (n == CLASSES - 1), early, recv1_sem.at[n])

        @pl.loop(n * per_class, (n + 1) * per_class, unroll=min(FORWARD_UNROLL, per_class))
        def _(k):
            forward(k, 0, early, 0)

        part = select(slice(n * per_class * 8, (n + 1) * per_class * 8), early_columns)
        if n == 0:
            total_ref[:, early_columns] = part
        else:
            total_ref[:, early_columns] += part

    place = {f: n for n, f in enumerate(EARLY + LATE)}

    def bottom_of(fields):
        return {f: total_ref[:, place[f] * cells : (place[f] + 1) * cells] for f in fields}

    bottom = bottom_of(EARLY)
    surface = [ocean_ref[:, f * cells : (f + 1) * cells] for f in range(4)]
    transfer, latent, fresh = freshwater_flux(bottom, surface)

    weighted = jnp.sum(area_ref[...] * fresh, axis=0, keepdims=True)
    total = jnp.sum(area_ref[...], axis=0, keepdims=True)
    half = cells // 2
    low_lanes = iota((1, cells), 1) < half
    sums = jnp.where(
        low_lanes, weighted + pltpu.roll(weighted, half, 1), total + pltpu.roll(total, half, 1)
    )
    zrows[pl.ds(region, 1), pl.ds(0, 1), :] = sums.reshape(1, 1, cells)

    def row_copy(source, target, send_sem, recv_sem, device):
        return pltpu.make_async_remote_copy(
            src_ref=source,
            dst_ref=target,
            send_sem=send_sem,
            recv_sem=recv_sem,
            device_id=device,
            device_id_type=MESH,
        )

    for r in range(roots):

        @pl.when(region != r)
        def _():
            row = zrows.at[region, pl.ds(0, 1)]
            row_copy(row, row, zsend_sem.at[r], zrecv_sem, (r, tile)).start()

    drain(recv1, tiles - 1, late, late_recv_sem)

    @pl.loop(0, chips, unroll=min(FORWARD_UNROLL, per_class))
    def _(k):
        forward(k, LATE_ROW, late, early)

    total_ref[:, late_columns] = select(slice(0, slots), late_columns)
    bottom.update(bottom_of(LATE))
    raw = fluxes(bottom, surface, transfer, latent, fresh)
    for f in range(nflx):
        if f != 6:
            ocean_out[:, f * cells : (f + 1) * cells] = raw[f]
    out_parts = [slice(0, 6 * cells), slice(7 * cells, nflx * cells), slice(6 * cells, 7 * cells)]
    stores = [
        pltpu.make_async_copy(ocean_out.at[:, p], ocean_hbm_out.at[:, p], out_sem.at[n])
        for n, p in enumerate(out_parts)
    ] + [pltpu.make_async_copy(atm_out, atm_hbm_out, out_sem.at[3])]
    stores[0].start()
    stores[1].start()
    fresh_high, fresh_low = two_parts(fresh)
    fields = [r.astype(BF16) for r in raw]
    fields[6] = fresh_high
    rows_back[...] = dot(feeds, jnp.concatenate(fields + [fresh_low], axis=1), ((0,), (0,)))
    ones = jnp.ones((8, cells), F32)

    def pair(a, b):
        upper = row8 < 4
        return jnp.where(upper, a, b) + pltpu.roll(jnp.where(upper, b, a), 4, 0)

    def four(a, b):
        near = row8 % 4 < 2
        x = jnp.where(near, b, a)
        return jnp.where(near, a, b) + jnp.where(near, pltpu.roll(x, 6, 0), pltpu.roll(x, 2, 0))

    def backward(k):
        g = chip_at(k, -1)
        at_rows = pl.ds(pl.multiple_of(k * 8, 8), 8)
        rows = [rows_back[at_rows, f * cells : (f + 1) * cells] for f in range(nflx + 1)]
        left = jnp.concatenate(rows + [ones], axis=0).astype(BF16)
        out = dot(left, group(g), ((1,), (1,)))
        x = []
        for f in range(nflx + 1):
            piece = out[f * 8 : (f + 1) * 8]
            mixed = jnp.where(even, piece[:, :cells], piece[:, cells:])
            x.append(jnp.where(own_lanes, mixed, 0.0))
        x[6] = x[6] + x[nflx]
        q0 = four(pair(x[0], x[4]), pair(x[2], x[6]))
        q1 = four(pair(x[1], x[5]), pair(x[3], x[7]))
        send2[g * 2, pl.ds(0, 8), :] = jnp.where(even, q0, pltpu.roll(q1, 1, 0))
        send2[g * 2 + 1, pl.ds(0, 8), :] = jnp.where(even, pltpu.roll(q0, 7, 0), q1)
        for h in range(2):
            at = (nflx + 1) * 8
            send2[g * 2 + h, pl.ds(nflx, 1), :] = out[at : at + 1, h * cells : (h + 1) * cells]

    def send_back(k):
        chip = chip_at(k, -1)
        for peer in (chip * 2 + core, chip * 2 + 1 - core):
            send(send2, recv2, (0, nflx + 1), send2_sem, recv2_sem, peer)

    whole_steps = (chips - 1) // BACK_STEP

    @pl.loop(0, whole_steps)
    def _(i):
        for u in range(BACK_STEP):
            backward(i * BACK_STEP + u)
        for u in range(BACK_STEP):
            send_back(i * BACK_STEP + u)

    for k in range(whole_steps * BACK_STEP, chips):
        backward(k)
    for k in range(whole_steps * BACK_STEP, chips - 1):
        send_back(k)
    send(send2, recv2, (0, nflx + 1), send2_sem, recv2_sem, my_chip * 2 + 1 - core)
    recv2[pl.ds(tile, 1), pl.ds(0, nflx + 1), :] = send2[pl.ds(tile, 1), pl.ds(0, nflx + 1), :]

    @pl.when(is_root)
    def _():
        if regions > 1:
            drain(zrows, regions - 1, 1, zrecv_sem)
        column = jnp.sum(zrows[:, 0, :], axis=0, keepdims=True)
        trows[pl.ds(tile, 1), pl.ds(0, 1), :] = column.reshape(1, 1, cells)

        def send_sums(_, peer):
            row = trows.at[tile, pl.ds(0, 1)]
            row_copy(row, row, tsend_sem, trecv_sem, (region, peer)).start()

        peers(send_sums)

    drain(recv2, tiles - 1, nflx + 1, recv2_sem)
    lane_group = iota((atm_blocks, cells), 1) // columns

    def gather(rows):
        found = dot(pick[: cap * atm_blocks], jnp.concatenate(rows, axis=1).astype(BF16))
        outs = []
        for n in range(len(rows)):
            x = jnp.zeros((atm_blocks, cells), F32)
            for c in range(cap):
                x = jnp.where(
                    lane_group == c,
                    found[c * atm_blocks : (c + 1) * atm_blocks, n * cells : (n + 1) * cells],
                    x,
                )
            x = x + pltpu.roll(x, 2 * columns, 1)
            outs.append(x + pltpu.roll(x, columns, 1))
        return outs

    outs = gather([recv2[:, f, :] for f in range(nflx) if f != 6])
    outs.insert(6, None)

    @pl.when(is_root)
    def _():
        drain(trows, tiles - 1, 1, trecv_sem)
        everything = jnp.sum(trows[:, 0, :], axis=0, keepdims=True)
        zmean[1, pl.ds(0, 1), :] = everything

    if regions > roots:

        @pl.when(jnp.logical_not(is_root))
        def _():
            drain(zmean, 1, 1, mrecv_sem)

        def send_mean(peer):
            mean = zmean.at[1, pl.ds(0, 1)]
            row_copy(mean, mean, msend_sem, mrecv_sem, (peer, tile)).start()

        @pl.when(region == 0)
        def _():
            @pl.loop(roots, near)
            def _(r):
                send_mean(r)

        @pl.when(hands_on)
        def _():
            send_mean(region + stride)

    sums_all = zmean[1, pl.ds(0, 1), :]
    weighted_all = jnp.sum(jnp.where(low_lanes, sums_all, 0.0), axis=1, keepdims=True)
    area_all = jnp.sum(jnp.where(low_lanes, 0.0, sums_all), axis=1, keepdims=True)
    shift = weighted_all / area_all
    ocean_out[:, 6 * cells : 7 * cells] = fresh - shift
    stores[2].start()
    outs[6] = gather([recv2[:, 6, :] - shift * recv2[:, nflx, :]])[0]
    for t in range(nflx // cap):
        x = outs[t * cap]
        for c in range(1, cap):
            x = jnp.where(lane_group == c, outs[t * cap + c], x)
        atm_out[:, t * cells : (t + 1) * cells] = x
    stores[3].start()

    drain(send1, tiles - 1, early, send1_sem)
    drain(send1, tiles - 1, late, late_send_sem)
    drain(send2, tiles - 1, nflx + 1, send2_sem)
    for r in range(roots):

        @pl.when(region != r)
        def _():
            drain(zrows, 1, 1, zsend_sem.at[r])

    @pl.when(is_root)
    def _():
        drain(trows, tiles - 1, 1, tsend_sem)

    if regions > roots:
        if near > roots:

            @pl.when(region == 0)
            def _():
                drain(zrows, near - roots, 1, msend_sem)

        @pl.when(hands_on)
        def _():
            drain(zrows, 1, 1, msend_sem)

    for store in stores:
        store.wait()


def copy_out(ocean_in, atm_in, ocean_out, atm_out, ocean_held, atm_held, sem):
    def both(first, second):
        copies = [
            pltpu.make_async_copy(source, target, sem.at[n])
            for n, (source, target) in enumerate(zip(first, second))
        ]
        for copy in copies:
            copy.start()
        for copy in copies:
            copy.wait()

    held = (ocean_held, atm_held)
    both((ocean_in, atm_in), held)
    both(held, (ocean_out, atm_out))


def per_device(
    regions, tiles, atm_state, ocean_state, cell_area, level_weights, remap, send_src, recv_ocn
):
    cap = send_src.shape[2]
    slots = tiles * cap
    atm_blocks = atm_state.shape[0]
    ocean_blocks, cells = cell_area.shape
    columns = remap.shape[1]
    nf = atm_state.shape[1] // cells
    nflx = 8
    hbm = pl.BlockSpec(memory_space=pl.ANY)
    box = pltpu.VMEM((tiles, 16, cells), F32)
    dma = pltpu.SemaphoreType.DMA
    results = (
        jax.ShapeDtypeStruct((ocean_blocks, nflx * cells), F32),
        jax.ShapeDtypeStruct((atm_blocks, nflx * columns), F32),
    )
    made = pl.pallas_call(
        functools.partial(kernel, regions, tiles),
        out_shape=results,
        in_specs=[hbm, hbm, hbm, pl.BlockSpec(memory_space=pltpu.SMEM), hbm, hbm, hbm],
        out_specs=(hbm, hbm),
        scratch_shapes=[
            pltpu.VMEM(atm_state.shape, BF16),
            pltpu.VMEM(ocean_state.shape, F32),
            pltpu.VMEM(cell_area.shape, F32),
            pltpu.VMEM((1, cap, tiles), jnp.int32),
            pltpu.VMEM((1, cap, tiles), jnp.int32),
            pltpu.VMEM(results[0].shape, F32),
            pltpu.VMEM(results[1].shape, F32),
            pltpu.VMEM((slots * columns, cells), BF16),
            box,
            box,
            pltpu.VMEM((slots, nf * cells), F32),
            pltpu.VMEM((ocean_blocks, nf * cells), F32),
            pltpu.VMEM((slots, (nflx + 1) * cells), F32),
            box,
            box,
            pltpu.VMEM((tiles, 8, cells), F32),
            pltpu.VMEM((regions, 8, cells), F32),
            pltpu.VMEM((2, 8, cells), F32),
            pltpu.SemaphoreType.DMA((6,)),
            dma,
            pltpu.SemaphoreType.DMA((CLASSES,)),
            dma, dma, dma, dma,
            pltpu.SemaphoreType.DMA((ROOTS,)),
            dma, dma, dma, dma, dma,
            pltpu.SemaphoreType.DMA((4,)),
        ],
        compiler_params=pltpu.CompilerParams(
            collective_id=0, has_side_effects=True, vmem_limit_bytes=60 * 1024 * 1024
        ),
        cost_estimate=pl.CostEstimate(
            flops=400_000_000, bytes_accessed=4_000_000, transcendentals=100_000
        ),
        name="couple",
    )(
        atm_state, ocean_state, cell_area, level_weights,
        remap.reshape(slots * columns, cells),
        jnp.swapaxes(send_src, 1, 2), jnp.swapaxes(recv_ocn, 1, 2),
    )
    return pl.pallas_call(
        copy_out,
        out_shape=results,
        in_specs=[hbm, hbm],
        out_specs=(hbm, hbm),
        scratch_shapes=[
            pltpu.VMEM(results[0].shape, F32),
            pltpu.VMEM(results[1].shape, F32),
            pltpu.SemaphoreType.DMA((2,)),
        ],
        compiler_params=pltpu.CompilerParams(vmem_limit_bytes=60 * 1024 * 1024),
        name="results",
    )(*made)


def solution(mesh):
    in_specs = (
        P(("region", "tile"), None),
        P(("region", "tile"), None),
        P(("region", "tile"), None),
        P(),
        P(("region", "tile"), None, None),
        P(("region", "tile"), None, None),
        P(("region", "tile"), None, None),
    )
    out_specs = (P(("region", "tile"), None), P(("region", "tile"), None))
    return jax.shard_map(
        functools.partial(per_device, mesh.shape["region"], mesh.shape["tile"]),
        mesh=mesh,
        in_specs=in_specs,
        out_specs=out_specs,
        check_vma=False,
    )
```

time: 53.9 us -> 50 us (0.928)
  local copies, waits for them, and re-layouts: 2.99 us -> 0 us
  Pallas kernels: 50 us -> 49.1 us
    unnamed x2 -> x0, local copies, waits for them, and re-layouts: 2.99 us -> none
    pallas_call x1 -> x2, Pallas kernels: 50 us -> 49.1 us  [the longest x1 47.5 us: per_device(): pl.pallas_call(functools.partial(kernel, regions, tiles), out_shape=resul...]
where the time goes in v3:
time: 50 us; the launch traced here: 49.8 us
  Pallas kernels  49.1 us (98%)
  between operations  0.64 us (1%)
    pallas_call x1, Pallas kernels, per_device(): pl.pallas_call(functools.partial(kernel, regions, tiles), out_shape=resul...  47.5 us
    pallas_call x1, Pallas kernels, per_device(): pl.pallas_call(copy_out, out_shape=results, in_specs=[hbm, hbm], out_spec...  1.67 us

profile of v3, /device:TPU:1, one launch (start us, length us, event | category | flops | bytes accessed | tf_op | source)
XLA Modules:
  0.0 49.8 jit_solution(9604310125583204500)
XLA Ops:
  0.6 47.5 %couple.1 = (f32[64,1024]{1,0:T(8,128)}, f32[16,256]{1,0:T(8,128)}) custom-call(bf16[16,1280]{1,0:T(8,128)(2,1)} %atm_hbm.1, f32[64,512]{1,0:T(8,128)} %ocean_hbm.1, f32[64,128]{1,0:T(8,128)} %area_hbm.1, f32[4]{0:T(128)} %weights_ref.1, bf16[8192,128]{1,0:T(8,128)(2,1)} %bitcast.3, s32[1,4,64]{2,1,0:T(4,128)} %bitcast.4, s32[1,4,64]{2,1,0:T(4,128)} %bitcast.5), custom_call_target="tpu_custom_call" | custom-call | flops 400000000 | bytes 4000000 | tf_op jit(solution)/shard_map/couple/pallas_call | solution.py:516
  48.1 1.7 %results.1 = (f32[64,1024]{1,0:T(8,128)}, f32[16,256]{1,0:T(8,128)}) custom-call(f32[64,1024]{1,0:T(8,128)} %get-tuple-element.4.ocean_in, f32[16,256]{1,0:T(8,128)} %get-tuple-element.5.atm_in), custom_call_target="tpu_custom_call" | custom-call | tf_op jit(solution)/shard_map/results/pallas_call | solution.py:560

commit v4 on v3

--- a/solution.py
+++ b/solution.py
@@ -16,7 +16,8 @@
 ROOTS = 2
 EARLY = (0, 1, 3, 6, 7, 8, 9)
 LATE = (2, 4, 5)
-LATE_ROW = 8
+STEPS = 32766.0
+LATE_ROW = 4
 
 
 def iota(shape, axis):
@@ -133,8 +134,9 @@
     is_root = region < roots
     hands_on = (region >= near - stride) & (region < regions - stride) & (near < regions)
     greeted = jnp.where(is_root, regions - 1, 1)
+    teller = roots - 1
     reached = jnp.where(
-        region == 0, near - 1, jnp.where(is_root, roots - 1, roots)
+        is_root, jnp.where(region == teller, near - 1, roots - 1), roots
     ) + hands_on.astype(jnp.int32)
 
     if regions > 1:
@@ -142,7 +144,7 @@
         @pl.loop(0, greeted)
         def _(i):
             apart = (region + outward(i, regions) + regions) % regions
-            giver = jnp.where(region < near, 0, region - stride)
+            giver = jnp.where(region < near, teller, region - stride)
             peer = jnp.where(is_root, apart, giver)
             pl.semaphore_signal(barrier, inc=1, device_id=(peer, tile), device_id_type=MESH)
 
@@ -179,10 +181,17 @@
     pick = jnp.where(wanted == at % atm_blocks, 1.0, 0.0).astype(BF16)
     packed = dot(pick, table, ((0,), (0,)))
     early, late = len(EARLY), len(LATE)
-    early_rows, late_rows = (0, early), (LATE_ROW, late)
+    early_words, late_words = early // 2 + 1, late // 2 + 1
+    early_rows, late_rows = (0, early_words), (LATE_ROW, late_words)
+    largest = jnp.max(jnp.abs(combined), axis=1, keepdims=True)
+    largest = jnp.max(largest, axis=0, keepdims=True)
+    power = jnp.floor(jnp.log2(jnp.maximum(largest, 1e-30))) + 1.0
+    whole = jnp.floor(packed * (STEPS * jnp.exp2(-power)) + 0.5).astype(jnp.int32)
+    power = jnp.broadcast_to(power.astype(jnp.int32), (tiles, cells))
     for start, fields in ((0, EARLY), (LATE_ROW, LATE)):
-        for n, f in enumerate(fields):
-            send1[:, start + n, :] = packed[:, f * cells : (f + 1) * cells]
+        parts_of = [whole[:, f * cells : (f + 1) * cells] for f in fields] + [power]
+        for n in range(len(parts_of) // 2):
+            send1[:, start + n, :] = parts_of[2 * n] * 65536 + (parts_of[2 * n + 1] + 32768)
 
     at = iota((tiles, slots), 1)
     sender = chip_at(at // 8, -1) * 2 + at % 2
@@ -214,7 +223,7 @@
         pltpu.make_async_copy(whole, whole, sem).wait()
 
     peers(lambda n, peer: send(send1, recv1, early_rows, send1_sem, recv1_sem.at[n], peer))
-    peers(lambda n, peer: send(send1, recv1, late_rows, late_send_sem, late_recv_sem, peer))
+    peers(lambda n, peer: send(send1, recv1, late_rows, late_send_sem, late_recv_sem.at[n], peer))
 
     for load in loads[3:]:
         load.wait()
@@ -232,13 +241,18 @@
         g = chip_at(k, -1)
         halves = []
         for h in range(2):
+            values = []
+            for n in range(rows_in // 2 + 1):
+                word = recv1[g * 2 + h, pl.ds(start + n, 1), :]
+                values += [word >> 16, (word & 65535) - 32768]
+            scale = jnp.exp2(values[rows_in].astype(F32)) * (1.0 / STEPS)
             rows = [
                 jnp.where(
                     diagonal[h],
-                    jnp.broadcast_to(recv1[g * 2 + h, pl.ds(start + f, 1), :], (8, cells)),
+                    jnp.broadcast_to(value.astype(F32) * scale, (8, cells)),
                     0.0,
                 )
-                for f in range(rows_in)
+                for value in values[:rows_in]
             ]
             halves.append(jnp.concatenate(rows, axis=0))
         high, low = two_parts(jnp.concatenate(halves, axis=1))
@@ -256,7 +270,7 @@
 
     early_columns, late_columns = slice(0, early * cells), slice(early * cells, nf * cells)
     for n in range(CLASSES):
-        drain(recv1, 2 * per_class - (n == CLASSES - 1), early, recv1_sem.at[n])
+        drain(recv1, 2 * per_class - (n == CLASSES - 1), early_words, recv1_sem.at[n])
 
         @pl.loop(n * per_class, (n + 1) * per_class, unroll=min(FORWARD_UNROLL, per_class))
         def _(k):
@@ -303,11 +317,12 @@
             row = zrows.at[region, pl.ds(0, 1)]
             row_copy(row, row, zsend_sem.at[r], zrecv_sem, (r, tile)).start()
 
-    drain(recv1, tiles - 1, late, late_recv_sem)
-
-    @pl.loop(0, chips, unroll=min(FORWARD_UNROLL, per_class))
-    def _(k):
-        forward(k, LATE_ROW, late, early)
+    for n in range(CLASSES):
+        drain(recv1, 2 * per_class - (n == CLASSES - 1), late_words, late_recv_sem.at[n])
+
+        @pl.loop(n * per_class, (n + 1) * per_class, unroll=min(FORWARD_UNROLL, per_class))
+        def _(k):
+            forward(k, LATE_ROW, late, early)
 
     total_ref[:, late_columns] = select(slice(0, slots), late_columns)
     bottom.update(bottom_of(LATE))
@@ -428,7 +443,7 @@
             mean = zmean.at[1, pl.ds(0, 1)]
             row_copy(mean, mean, msend_sem, mrecv_sem, (peer, tile)).start()
 
-        @pl.when(region == 0)
+        @pl.when(region == teller)
         def _():
             @pl.loop(roots, near)
             def _(r):
@@ -452,8 +467,8 @@
         atm_out[:, t * cells : (t + 1) * cells] = x
     stores[3].start()
 
-    drain(send1, tiles - 1, early, send1_sem)
-    drain(send1, tiles - 1, late, late_send_sem)
+    drain(send1, tiles - 1, early_words, send1_sem)
+    drain(send1, tiles - 1, late_words, late_send_sem)
     drain(send2, tiles - 1, nflx + 1, send2_sem)
     for r in range(roots):
 
@@ -468,7 +483,7 @@
     if regions > roots:
         if near > roots:
 
-            @pl.when(region == 0)
+            @pl.when(region == teller)
             def _():
                 drain(zrows, near - roots, 1, msend_sem)
 
@@ -527,8 +542,8 @@
             pltpu.VMEM(results[0].shape, F32),
             pltpu.VMEM(results[1].shape, F32),
             pltpu.VMEM((slots * columns, cells), BF16),
-            box,
-            box,
+            pltpu.VMEM((tiles, 8, cells), jnp.int32),
+            pltpu.VMEM((tiles, 8, cells), jnp.int32),
             pltpu.VMEM((slots, nf * cells), F32),
             pltpu.VMEM((ocean_blocks, nf * cells), F32),
             pltpu.VMEM((slots, (nflx + 1) * cells), F32),
@@ -542,7 +557,8 @@
             pltpu.SemaphoreType.DMA((CLASSES,)),
             dma, dma, dma, dma,
             pltpu.SemaphoreType.DMA((ROOTS,)),
-            dma, dma, dma, dma, dma,
+            dma, dma, dma, dma,
+            pltpu.SemaphoreType.DMA((CLASSES,)),
             pltpu.SemaphoreType.DMA((4,)),
         ],
         compiler_params=pltpu.CompilerParams(

time: 50 us -> 48.7 us (0.974)
  Pallas kernels: 49.1 us -> 47.9 us
    pallas_call x1, Pallas kernels: 47.5 us -> 46.2 us  [per_device(): pl.pallas_call(functools.partial(kernel, regions, tiles), out_shape=resul...]
where the time goes in v4:
time: 48.7 us; the launch traced here: 48.5 us
  Pallas kernels  47.9 us (98%)
  between operations  0.64 us (1%)
    pallas_call x1, Pallas kernels, per_device(): pl.pallas_call(functools.partial(kernel, regions, tiles), out_shape=resul...  46.2 us
    pallas_call x1, Pallas kernels, per_device(): pl.pallas_call(copy_out, out_shape=results, in_specs=[hbm, hbm], out_spec...  1.67 us

profile of v4, /device:TPU:1, one launch (start us, length us, event | category | flops | bytes accessed | tf_op | source)
XLA Modules:
  0.0 48.5 jit_solution(14475843421595367577)
XLA Ops:
  0.6 46.2 %couple.1 = (f32[64,1024]{1,0:T(8,128)}, f32[16,256]{1,0:T(8,128)}) custom-call(bf16[16,1280]{1,0:T(8,128)(2,1)} %atm_hbm.1, f32[64,512]{1,0:T(8,128)} %ocean_hbm.1, f32[64,128]{1,0:T(8,128)} %area_hbm.1, f32[4]{0:T(128)} %weights_ref.1, bf16[8192,128]{1,0:T(8,128)(2,1)} %bitcast.3, s32[1,4,64]{2,1,0:T(4,128)} %bitcast.4, s32[1,4,64]{2,1,0:T(4,128)} %bitcast.5), custom_call_target="tpu_custom_call" | custom-call | flops 400000000 | bytes 4000000 | tf_op jit(solution)/shard_map/couple/pallas_call | solution.py:531
  46.9 1.7 %results.1 = (f32[64,1024]{1,0:T(8,128)}, f32[16,256]{1,0:T(8,128)}) custom-call(f32[64,1024]{1,0:T(8,128)} %get-tuple-element.4.ocean_in, f32[16,256]{1,0:T(8,128)} %get-tuple-element.5.atm_in), custom_call_target="tpu_custom_call" | custom-call | tf_op jit(solution)/shard_map/results/pallas_call | solution.py:576

commit v5 on v4

--- a/solution.py
+++ b/solution.py
@@ -14,6 +14,7 @@
 FORWARD_UNROLL = 4
 BACK_STEP = 4
 ROOTS = 2
+PIECES = 4
 EARLY = (0, 1, 3, 6, 7, 8, 9)
 LATE = (2, 4, 5)
 STEPS = 32766.0
@@ -425,7 +426,9 @@
         return outs
 
     outs = gather([recv2[:, f, :] for f in range(nflx) if f != 6])
-    outs.insert(6, None)
+    exact = [x.astype(F32) for f in (6, nflx) for x in two_parts(recv2[:, f, :])]
+    fresh_high, fresh_low, ones_high, ones_low = gather(exact)
+    fresh_back, ones_back = fresh_high + fresh_low, ones_high + ones_low
 
     @pl.when(is_root)
     def _():
@@ -459,7 +462,7 @@
     shift = weighted_all / area_all
     ocean_out[:, 6 * cells : 7 * cells] = fresh - shift
     stores[2].start()
-    outs[6] = gather([recv2[:, 6, :] - shift * recv2[:, nflx, :]])[0]
+    outs.insert(6, fresh_back - shift * ones_back)
     for t in range(nflx // cap):
         x = outs[t * cap]
         for c in range(1, cap):
@@ -496,19 +499,26 @@
 
 
 def copy_out(ocean_in, atm_in, ocean_out, atm_out, ocean_held, atm_held, sem):
-    def both(first, second):
-        copies = [
-            pltpu.make_async_copy(source, target, sem.at[n])
-            for n, (source, target) in enumerate(zip(first, second))
-        ]
-        for copy in copies:
-            copy.start()
-        for copy in copies:
-            copy.wait()
-
-    held = (ocean_held, atm_held)
-    both((ocean_in, atm_in), held)
-    both(held, (ocean_out, atm_out))
+    height = ocean_in.shape[0] // PIECES
+    legs = [(atm_in, atm_held, atm_out)]
+    for n in range(PIECES):
+        rows = pl.ds(n * height, height)
+        legs.append((ocean_in.at[rows], ocean_held.at[rows], ocean_out.at[rows]))
+    arrivals = [
+        pltpu.make_async_copy(source, held, sem.at[0, n])
+        for n, (source, held, _) in enumerate(legs)
+    ]
+    leaves = [
+        pltpu.make_async_copy(held, target, sem.at[1, n])
+        for n, (_, held, target) in enumerate(legs)
+    ]
+    for arrival in arrivals:
+        arrival.start()
+    for arrival, leave in zip(arrivals, leaves):
+        arrival.wait()
+        leave.start()
+    for leave in leaves:
+        leave.wait()
 
 
 def per_device(
@@ -581,7 +591,7 @@
         scratch_shapes=[
             pltpu.VMEM(results[0].shape, F32),
             pltpu.VMEM(results[1].shape, F32),
-            pltpu.SemaphoreType.DMA((2,)),
+            pltpu.SemaphoreType.DMA((2, PIECES + 1)),
         ],
         compiler_params=pltpu.CompilerParams(vmem_limit_bytes=60 * 1024 * 1024),
         name="results",

time: 48.7 us -> 48.5 us (level)
  no operation moved by 1% of the time
where the time goes in v5:
time: 48.5 us; the launch traced here: 48.2 us
  Pallas kernels  47.6 us (98%)
  between operations  0.64 us (1%)
    pallas_call x1, Pallas kernels, per_device(): pl.pallas_call(functools.partial(kernel, regions, tiles), out_shape=resul...  45.9 us
    pallas_call x1, Pallas kernels, per_device(): pl.pallas_call(copy_out, out_shape=results, in_specs=[hbm, hbm], out_spec...  1.67 us

profile of v5, /device:TPU:1, one launch (start us, length us, event | category | flops | bytes accessed | tf_op | source)
XLA Modules:
  0.0 48.2 jit_solution(5689054029513438054)
XLA Ops:
  0.6 45.9 %couple.1 = (f32[64,1024]{1,0:T(8,128)}, f32[16,256]{1,0:T(8,128)}) custom-call(bf16[16,1280]{1,0:T(8,128)(2,1)} %atm_hbm.1, f32[64,512]{1,0:T(8,128)} %ocean_hbm.1, f32[64,128]{1,0:T(8,128)} %area_hbm.1, f32[4]{0:T(128)} %weights_ref.1, bf16[8192,128]{1,0:T(8,128)(2,1)} %bitcast.3, s32[1,4,64]{2,1,0:T(4,128)} %bitcast.4, s32[1,4,64]{2,1,0:T(4,128)} %bitcast.5), custom_call_target="tpu_custom_call" | custom-call | flops 400000000 | bytes 4000000 | tf_op jit(solution)/shard_map/couple/pallas_call | solution.py:541
  46.6 1.7 %results.1 = (f32[64,1024]{1,0:T(8,128)}, f32[16,256]{1,0:T(8,128)}) custom-call(f32[64,1024]{1,0:T(8,128)} %get-tuple-element.4.ocean_in, f32[16,256]{1,0:T(8,128)} %get-tuple-element.5.atm_in), custom_call_target="tpu_custom_call" | custom-call | tf_op jit(solution)/shard_map/results/pallas_call | solution.py:586
